TPU v7x, 256 devices: a whole 4x4x8 slice. The times are simulated.
256 devices in a mesh: grp: 8 (over z), seq: 32 (over y, x, core).
Axes of the slice: x: 4, y: 4, z: 8, core: 2. Of those that a mesh axis runs over, the one named last changes fastest.
Arguments:
- loader_layer_input: bfloat16 [32768, 8192], P('seq', 'grp'), may hold values from -6 to 6
- loader_output_gradient: bfloat16 [32768, 2048], P('seq', 'grp'), may hold values from -0.049804688 to 0.049804688
- trial_per_block: int32 [1024, 1], P('seq'), may hold values from 0 to 31; in each aligned block of 32 rows (0 to 31, 32 to 63, ...) at most 2 rows name the same one
- trial_slot_index: int32 [32], replicated, may hold values from 0 to 31, each once
- frozen_weight: bfloat16 [8192, 2048], P('grp'), may hold values from -0.0625 to 0.0625
- down_adapters: bfloat16 [32, 8192, 64], P(None, 'grp'), may hold values from -0.0625 to 0.0625
- up_adapters: bfloat16 [32, 64, 2048], P(None, None, 'grp'), may hold values from -0.75 to 0.75
Outputs:
- output: bfloat16 [32768, 2048], P('seq', 'grp')
- down_adapter_gradient: float32 [32, 8192, 64], P('seq', 'grp')
- up_adapter_gradient: float32 [32, 64, 2048], P('seq', None, 'grp')
Inputs may be any that keep to these rules, and one draw needn't show every extreme that they name: `trial_per_block`: in every aligned group of 32 rows (one data shard's blocks) no trial appears more than 2 times. `trial_slot_index`: A permutation of the trials; slot k is held by index k // 1 of seq.
All inputs are finite; a program needn't handle non-finite values.
Results may differ from a plain program's by a relative error of at most 0.0046.
Values may be sent and summed in bfloat16 or wider, within the bound.
A program may use at most 128 MiB of HBM per device.

v0:
```python
import jax
import jax.numpy as jnp
from jax import lax
from jax.sharding import PartitionSpec as P

ADAPTER_SCALE = 2.0


def block_rows(values, blocks):
    return values.reshape(blocks, values.shape[0] // blocks, values.shape[1])


def slot_lookup(trial_index_list, trial_slot_index):
    trial_list = trial_slot_index.shape[0]
    match = trial_index_list[:, None] == jnp.arange(trial_list, dtype=jnp.int32)[None, :]
    return jnp.sum(jnp.where(match, trial_slot_index[None, :], 0), axis=1)


def local_forward_backward(
    input_row_list, gradient_row_list, trial_row_list, frozen_weight, down_adapters, up_adapters
):
    blocks = trial_row_list.shape[0]
    trial_index_list = trial_row_list[:, 0]
    input_block_list = block_rows(input_row_list, blocks)
    gradient_block_list = block_rows(gradient_row_list, blocks)
    down_projected_blocks = jnp.take(down_adapters, trial_index_list, axis=0)
    up_projected_blocks = jnp.take(up_adapters, trial_index_list, axis=0)
    down_part = jnp.einsum(
        "xha,xau->xhu", input_block_list, down_projected_blocks, preferred_element_type=jnp.float32
    )
    back_part = jnp.einsum(
        "bkf,brf->bkr", gradient_block_list, up_projected_blocks, preferred_element_type=jnp.float32
    )
    partial_terms = jnp.dot(input_row_list, frozen_weight, preferred_element_type=jnp.float32)
    frozen_output = lax.psum_scatter(partial_terms, "grp", scatter_dimension=1, tiled=True)
    down_total, backward_total = lax.psum((down_part, back_part), "grp")
    adapter_down_projection = down_total.astype(jnp.bfloat16)
    adapter_backward = backward_total.astype(jnp.bfloat16)
    adapter_branch = jnp.einsum(
        "lts,lsd->ltd",
        adapter_down_projection,
        up_projected_blocks,
        preferred_element_type=jnp.float32,
    )
    combined_output = (
        frozen_output + ADAPTER_SCALE * adapter_branch.reshape(frozen_output.shape)
    ).astype(jnp.bfloat16)
    return (
        combined_output,
        adapter_down_projection,
        adapter_backward,
        input_block_list,
        gradient_block_list,
    )


def dense_contributions(
    input_block_list,
    gradient_block_list,
    adapter_down_projection,
    adapter_backward,
    slot_index_list,
    trial_list,
):
    down_block_grad = jnp.einsum(
        "afq,afe->aqe", input_block_list, adapter_backward, preferred_element_type=jnp.float32
    )
    up_block_grad = jnp.einsum(
        "vjo,vjt->vot",
        adapter_down_projection,
        gradient_block_list,
        preferred_element_type=jnp.float32,
    )
    down_dense_grad = (
        jnp.zeros((trial_list,) + down_block_grad.shape[1:], jnp.float32)
        .at[slot_index_list]
        .add(down_block_grad)
    )
    up_dense_grad = (
        jnp.zeros((trial_list,) + up_block_grad.shape[1:], jnp.float32)
        .at[slot_index_list]
        .add(up_block_grad)
    )
    return (down_dense_grad, up_dense_grad)


def local(
    loader_layer_input,
    loader_output_gradient,
    trial_per_block,
    trial_slot_index,
    frozen_weight,
    down_adapters,
    up_adapters,
):
    trial_list = trial_slot_index.shape[0]
    input_row_list, gradient_row_list, trial_row_list = (
        lax.all_to_all(loader_layer_input, "seq", split_axis=0, concat_axis=0, tiled=True),
        lax.all_to_all(loader_output_gradient, "seq", split_axis=0, concat_axis=0, tiled=True),
        lax.all_to_all(trial_per_block, "seq", split_axis=0, concat_axis=0, tiled=True),
    )
    (
        combined_output,
        adapter_down_projection,
        adapter_backward,
        input_block_list,
        gradient_block_list,
    ) = local_forward_backward(
        input_row_list, gradient_row_list, trial_row_list, frozen_weight, down_adapters, up_adapters
    )
    slot_index_list = slot_lookup(trial_row_list[:, 0], trial_slot_index)
    down_dense_grad, up_dense_grad = dense_contributions(
        input_block_list,
        gradient_block_list,
        adapter_down_projection,
        adapter_backward,
        slot_index_list,
        trial_list,
    )
    down_gradient_total, up_gradient_total = (
        lax.psum_scatter(down_dense_grad, "seq", scatter_dimension=0, tiled=True),
        lax.psum_scatter(up_dense_grad, "seq", scatter_dimension=0, tiled=True),
    )
    return (combined_output, ADAPTER_SCALE * down_gradient_total, ADAPTER_SCALE * up_gradient_total)


def solution(mesh):
    in_specs = (
        P("seq", "grp"),
        P("seq", "grp"),
        P("seq", None),
        P(),
        P("grp", None),
        P(None, "grp", None),
        P(None, None, "grp"),
    )
    out_specs = (P("seq", "grp"), P("seq", "grp", None), P("seq", None, "grp"))
    return jax.shard_map(local, mesh=mesh, in_specs=in_specs, out_specs=out_specs, check_vma=False)
```

profile of v0, /device:TPU:1, one launch (start us, length us, event | category | flops | bytes accessed | tf_op | source)
XLA Modules:
  0.0 442.3 jit_solution(5799644423290264488)
XLA Ops:
  7.2 0.0 copy-start
  7.2 0.8 copy.12
  8.0 15.3 %all_to_all.36 = s32[32,1,1]{2,1,0:T(1,128)S(1)} all-to-all(s32[32,1,1]{2,1,0:T(1,128)S(1)} %copy.12), channel_id=1, replica_groups=mesh['grp'=8,'seq'=32] {'seq'}, dimensions={0} | all-to-all | bytes 256 | tf_op jit(solution)/shard_map/all_to_all | solution.py:100
  23.3 16.5 %all_to_all.37 = bf16[32,32,256]{2,1,0:T(8,128)(2,1)} all-to-all(bf16[32,32,256]{2,1,0:T(8,128)(2,1)} %bitcast.33), channel_id=1, replica_groups=mesh['grp'=8,'seq'=32] {'seq'}, dimensions={0} | all-to-all | bytes 1048576 | tf_op jit(solution)/shard_map/all_to_all | solution.py:99
  39.9 4.1 all-to-all-start
  44.0 0.0 reduce-scatter.8.cloned.1.call-start
  44.0 0.7 reduce
  44.7 0.0 copy-done
  44.7 1.6 gather_fusion.1
  46.3 0.0 copy-start.5
  46.3 4.9 %gather_fusion = bf16[32,1024,64]{1,2,0:T(8,128)(2,1)} fusion(bf16[32,1024,64]{1,2,0:T(8,128)(2,1)} %param.12, s32[1024]{0:T(1024)S(1)} %pad_clamp_fusion), kind=kCustom, calls=%fused_computation | custom fusion | bytes 8388736 | tf_op jit(solution)/shard_map/jit(_take)/gather | solution.py:26
  51.3 0.0 copy-done.5
  51.3 0.2 select_reduce_fusion
  51.5 2.7 convolution_bitcast_fusion.1
  54.1 17.8 %all-to-all-done = bf16[32,32,1024]{2,1,0:T(8,128)(2,1)S(1)} async-done(((bf16[32,32,1024]{2,1,0:T(8,128)(2,1)}), bf16[32,32,1024]{2,1,0:T(8,128)(2,1)S(1)}, u32[]{:S(2)}, u32[]{:S(2)}) %all-to-all-start) | async-done | bytes 2097184 | tf_op jit(solution)/shard_map/all_to_all | solution.py:98
  71.9 0.0 copy-start.2
  71.9 5.0 %fusion.4 = f32[32,32,64]{2,1,0:T(8,128)} fusion(bf16[32,32,1024]{2,1,0:T(8,128)(2,1)S(1)} %all-to-all-done, bf16[32,1024,64]{1,2,0:T(8,128)(2,1)} %gather_fusion, pred[32]{0:T(512)(128)(4,1)S(1)} %compare_and_fusion), kind=kOutput, calls=%fused_computation.10 | convolution fusion | flops 136314880 | bytes 6553632 | tf_op jit(solution)/shard_map/xha,xau->xhu/dot_general | solution.py:28
  77.0 0.0 copy-done.2
  77.0 54.3 %all-reduce.2 = (bf16[32,32,64]{2,1,0:T(8,128)(2,1)S(1)}, bf16[32,32,64]{2,1,0:T(8,128)(2,1)}) all-reduce(f32[32,32,64]{2,1,0:T(8,128)} %fusion.4, f32[32,32,64]{2,1,0:T(8,128)} %convolution_bitcast_fusion.1), channel_id=1, replica_groups=mesh['grp'=8,'seq'=32] {'grp'}, use_global_device_ids=true, to_apply=%region_1.2 | all-reduce | flops 131072 | bytes 786432 | tf_op jit(solution)/shard_map/psum | solution.py:36
  131.2 2.9 fusion.18
  134.1 0.2 broadcast_in_dim.49
  134.3 4.7 %scatter_fusion.1 = f32[32,64,256]{2,1,0:T(8,128)S(1)} fusion(f32[32,64,256]{2,1,0:T(8,128)S(1)} %broadcast_in_dim.49, s32[32]{0:T(128)S(1)} %fusion.13, f32[32,64,256]{2,1,0:T(8,128)} %fusion.18), kind=kCustom, calls=%fused_computation.3 | custom fusion | flops 524288 | bytes 6291584 | tf_op jit(solution)/shard_map/scatter-add | solution.py:82
  139.0 0.0 copy-start.1
  139.0 1.3 copy-done.1
  140.3 0.0 reduce-scatter.8.cloned.1.call-update
  140.3 0.0 reduce-scatter.6.cloned.1.call-start
  140.4 6.2 %convolution_bitcast_fusion = f32[32,1024,64]{1,2,0:T(8,128)} fusion(bf16[32,32,1024]{2,1,0:T(8,128)(2,1)} %copy-done.2, bf16[32,32,64]{2,1,0:T(8,128)(2,1)} %get-tuple-element.4), kind=kOutput, calls=%fused_computation.7 | convolution fusion | flops 134217728 | bytes 10616832 | tf_op jit(solution)/shard_map/afq,afe->aqe/dot_general | solution.py:65
  146.6 4.3 broadcast_in_dim.46
  150.9 18.9 %scatter_fusion = f32[32,1024,64]{1,2,0:T(8,128)} fusion(f32[32,1024,64]{1,2,0:T(8,128)} %broadcast_in_dim.46, s32[32]{0:T(128)S(1)} %fusion.13, f32[32,1024,64]{1,2,0:T(8,128)} %convolution_bitcast_fusion), kind=kCustom, calls=%fused_computation.2 | custom fusion | flops 2097152 | bytes 25165952 | tf_op jit(solution)/shard_map/scatter-add | solution.py:77
  169.7 0.0 copy-start.3
  169.7 0.0 reduce-scatter.6.cloned.1.call-update
  169.8 0.0 reduce-scatter.4.cloned.1.call-start
  169.8 1.6 copy-done.3
  171.4 8.9 %fusion.17 = f32[1024,2048]{1,0:T(8,128)} fusion(bf16[1024,1024]{1,0:T(8,128)(2,1)S(1)} %bitcast.31, bf16[1024,2048]{1,0:T(8,128)(2,1)} %param.11), kind=kOutput, calls=%fused_computation.33 | convolution fusion | flops 4294967296 | bytes 14680064 | tf_op jit(solution)/shard_map/dot_general | solution.py:34
  180.3 0.0 copy-start.4
  180.3 0.0 reduce-scatter.4.cloned.1.call-update
  180.3 1.2 copy-done.4
  181.5 0.4 convolution_multiply_fusion
  181.9 49.1 %reduce-scatter.8.cloned.1.call-done = f32[1,64,256]{2,1,0:T(8,128)} async-done(((f32[32,64,256]{2,1,0:T(8,128)}), f32[1,64,256]{2,1,0:T(8,128)}) %reduce-scatter.8.cloned.1.call-update) | async-done | bytes 65552 | tf_op jit(solution)/shard_map/reduce_scatter | solution.py:122
  231.0 1.5 broadcast_multiply_fusion.1
  232.5 102.3 %reduce-scatter.6.cloned.1.call-done = f32[1,1024,64]{1,2,0:T(8,128)} async-done(((f32[32,1024,64]{1,2,0:T(8,128)}), f32[1,1024,64]{1,2,0:T(8,128)}) %reduce-scatter.6.cloned.1.call-update) | async-done | bytes 262160 | tf_op jit(solution)/shard_map/reduce_scatter | solution.py:121
  334.8 1.7 broadcast_multiply_fusion
  336.5 97.2 %reduce-scatter.4.cloned.1.call-done = f32[1024,256]{1,0:T(8,128)} async-done(((f32[1024,2048]{1,0:T(8,128)}), f32[1024,256]{1,0:T(8,128)}) %reduce-scatter.4.cloned.1.call-update) | async-done | bytes 1048592 | tf_op jit(solution)/shard_map/reduce_scatter | solution.py:35
  433.6 2.2 fusion.7
  (4 shorter events, 0.0 us)
Async XLA Ops:
  7.2 37.6 %copy-start = (bf16[32,64,256]{2,1,0:T(8,128)(2,1)S(1)}, bf16[32,64,256]{2,1,0:T(8,128)(2,1)}, u32[]{:S(2)}) copy-start(bf16[32,64,256]{2,1,0:T(8,128)(2,1)} %param.13) | copy-start | bytes 3145732
  39.9 32.1 %all-to-all-start = ((bf16[32,32,1024]{2,1,0:T(8,128)(2,1)}), bf16[32,32,1024]{2,1,0:T(8,128)(2,1)S(1)}, u32[]{:S(2)}, u32[]{:S(2)}) async-start(bf16[32,32,1024]{2,1,0:T(8,128)(2,1)} %bitcast.32), calls=%async_computation | async-start | bytes 4194304 | tf_op jit(solution)/shard_map/all_to_all | solution.py:98
  44.0 187.1 %reduce-scatter.8.cloned.1.call-start = ((), (), s32[]{:S(2)}) async-start(), calls=%async_computation.8 | async-start | bytes 2162688 | tf_op jit(solution)/shard_map/reduce_scatter | solution.py:122
  46.3 4.9 %copy-start.5 = (s32[32]{0:T(128)S(1)}, s32[32]{0:T(128)}, u32[]{:S(2)}) copy-start(s32[32]{0:T(128)} %param.10) | copy-start | bytes 388
  71.9 5.0 %copy-start.2 = (bf16[32,32,1024]{2,1,0:T(8,128)(2,1)}, bf16[32,32,1024]{2,1,0:T(8,128)(2,1)S(1)}, u32[]{:S(2)}) copy-start(bf16[32,32,1024]{2,1,0:T(8,128)(2,1)S(1)} %all-to-all-done) | copy-start | bytes 6291460
  139.0 1.3 copy-start.1
  140.3 194.4 %reduce-scatter.6.cloned.1.call-start = ((), (), s32[]{:S(2)}) async-start(), calls=%async_computation.7 | async-start | bytes 8650752 | tf_op jit(solution)/shard_map/reduce_scatter | solution.py:121
  169.7 1.6 copy-start.3
  169.8 263.8 %reduce-scatter.4.cloned.1.call-start = ((), (), s32[]{:S(2)}) async-start(), calls=%async_computation.6 | async-start | bytes 9437184 | tf_op jit(solution)/shard_map/reduce_scatter | solution.py:35
  180.3 1.2 copy-start.4
Sparse Core Ops, SparseCore 0:
  140.5 90.5 reduce-scatter.7
  235.1 99.6 reduce-scatter.5
  337.5 96.0 reduce-scatter.3
where the time goes:
time: 443 us; the launch traced here: 442 us
  waiting for transfers between devices  266 us (60%)
  blocking collectives  86.1 us (19%)
  other arithmetic  29.7 us (7%)
  matrix products  26 us (6%)
  local copies, waits for them, and re-layouts  15.9 us (4%)
  between operations  13.8 us (3%)
    reduce_scatter x1, waiting for transfers between devices, local(): lax.psum_scatter(down_dense_grad, 'seq', scatter_dimension=0, tiled=True)  102 us
    reduce_scatter x1, waiting for transfers between devices, local_forward_backward(): lax.psum_scatter(partial_terms, 'grp', scatter_dimension=1, tiled=True)  97.2 us
    psum x1, blocking collectives, local_forward_backward(): down_total, backward_total = lax.psum((down_part, back_part), 'grp')  54.3 us
    reduce_scatter x1, waiting for transfers between devices, local(): lax.psum_scatter(up_dense_grad, 'seq', scatter_dimension=0, tiled=True)  49.1 us
    scatter-add x1, other arithmetic, dense_contributions(): down_dense_grad = jnp.zeros((trial_list,) + down_block_grad.shape[1:], jn...  18.9 us
    all_to_all x1, waiting for transfers between devices, local(): lax.all_to_all(loader_layer_input, 'seq', split_axis=0, concat_axis=0, ti...  17.8 us
    all_to_all x1, blocking collectives, local(): lax.all_to_all(loader_output_gradient, 'seq', split_axis=0, concat_axis=0...  16.5 us
    all_to_all x1, blocking collectives, local(): lax.all_to_all(trial_per_block, 'seq', split_axis=0, concat_axis=0, tiled...  15.3 us
  transfers between devices with their start and end apart: 4, of which 4 were waited for; matrix products, arithmetic and copies ran while one was open for 12% of the time, Pallas kernels for 0%

commit v1 on v0

v1 whole, which is shorter than its diff:
```python
import jax
import jax.numpy as jnp
from jax import lax
from jax.sharding import PartitionSpec as P

ADAPTER_SCALE = 2.0


def local(x, g, trial_per_block, trial_slot_index, w, down, up):
    blocks = trial_per_block.shape[0]
    trials, depth, rank = down.shape
    cols = up.shape[2]
    blk = x.shape[0] // blocks
    trial = trial_per_block[:, 0]
    one_hot = (trial[:, None] == jnp.arange(trials, dtype=jnp.int32)[None, :]).astype(jnp.bfloat16)
    slot_hot = (trial_slot_index[:, None] == jnp.arange(trials, dtype=jnp.int32)[None, :]).astype(jnp.bfloat16)
    block_slot = jnp.dot(one_hot, slot_hot)
    xb = x.reshape(blocks, blk, depth)
    gb = g.reshape(blocks, blk, cols)
    down_b = jnp.einsum("bt,tfr->bfr", one_hot, down)
    up_b = jnp.einsum("bt,tro->bro", one_hot, up)
    down_part = jnp.einsum("bpf,bfr->bpr", xb, down_b, preferred_element_type=jnp.float32)
    back_part = jnp.einsum("bpo,bro->bpr", gb, up_b, preferred_element_type=jnp.float32)
    down_total, back_total = lax.psum((down_part, back_part), "grp")
    ld = down_total.astype(jnp.bfloat16)
    lb = back_total.astype(jnp.bfloat16)
    part = jnp.dot(x, w, preferred_element_type=jnp.float32)
    frozen = lax.psum_scatter(part, "grp", scatter_dimension=1, tiled=True)
    lb_all = (lb[:, :, None, :] * block_slot[:, None, :, None]).reshape(blocks * blk, trials * rank)
    ld_all = (ld[:, :, None, :] * block_slot[:, None, :, None]).reshape(blocks * blk, trials * rank)
    down_dense = jnp.einsum("nf,nq->qf", x, lb_all, preferred_element_type=jnp.float32)
    up_dense = jnp.einsum("nq,no->qo", ld_all, g, preferred_element_type=jnp.float32)
    both = jnp.concatenate([down_dense.reshape(trials, rank, depth), up_dense.reshape(trials, rank, cols)], axis=2)
    total = ADAPTER_SCALE * lax.psum_scatter(both, "seq", scatter_dimension=0, tiled=True)
    branch = jnp.einsum("bpr,bro->bpo", ld, up_b, preferred_element_type=jnp.float32)
    mixed = (frozen + ADAPTER_SCALE * branch.reshape(frozen.shape)).astype(jnp.bfloat16)
    out = lax.all_to_all(mixed, "seq", split_axis=0, concat_axis=0, tiled=True)
    return out, jnp.transpose(total[:, :, :depth], (0, 2, 1)), total[:, :, depth:]


def solution(mesh):
    in_specs = (
        P("seq", "grp"),
        P("seq", "grp"),
        P("seq", None),
        P(),
        P("grp", None),
        P(None, "grp", None),
        P(None, None, "grp"),
    )
    out_specs = (P("seq", "grp"), P("seq", "grp", None), P("seq", None, "grp"))
    return jax.shard_map(local, mesh=mesh, in_specs=in_specs, out_specs=out_specs, check_vma=False)
```

time: 443 us -> 301 us (0.68)
  waiting for transfers between devices: 266 us -> 90.7 us
  local copies, waits for them, and re-layouts: 15.9 us -> 41.8 us
  starting transfers between devices: 4.23 us -> 14.9 us
  matrix products: 26 us -> 36.6 us
  other arithmetic: 29.7 us -> 19.8 us
    reduce_scatter x3 -> x2, waiting for transfers between devices: 249 us -> 90.7 us  [the longest x1 90.7 us: local(): lax.psum_scatter(both, 'seq', scatter_dimension=0, tiled=True)]
    all_to_all x2 -> x0, blocking collectives: 31.9 us -> none  [the longest x1 16.5 us: local(): lax.all_to_all(loader_output_gradient, 'seq', split_axis=0, concat_axis=0...]
    psum x1, blocking collectives: 54.3 us -> 82.3 us  [local(): down_total, back_total = lax.psum((down_part, back_part), 'grp')]
    mul x0 -> x2, local copies, waits for them, and re-layouts: none -> 24.7 us  [the longest x1 12.3 us: local(): lb[:, :, None, :] * block_slot[:, None, :, None]]
    scatter-add x2 -> x0, other arithmetic: 23.5 us -> none  [the longest x1 18.9 us: dense_contributions(): down_dense_grad = jnp.zeros((trial_list,) + down_block_grad.shape[1:], jn...]
    all_to_all x1, waiting for transfers between devices: 17.8 us -> 0.01 us  [local(): out = lax.all_to_all(mixed, 'seq', split_axis=0, concat_axis=0, tiled=True)]
    dot_general x0 -> x2, local copies, waits for them, and re-layouts: none -> 12.8 us  [the longest x1 6.41 us: local(): jnp.einsum('nf,nq->qf', x, lb_all, preferred_element_type=jnp.float32)]
    all_to_all x1, starting transfers between devices: 4.11 us -> 14.8 us  [local(): out = lax.all_to_all(mixed, 'seq', split_axis=0, concat_axis=0, tiled=True)]
  transfers between devices with their start and end apart: 4 -> 3, of which waited for: 4 -> 1; matrix products, arithmetic and copies ran while one was open for 12% -> 29% of each run, Pallas kernels for 0% -> 0%
where the time goes in v1:
time: 301 us; the launch traced here: 300 us
  waiting for transfers between devices  90.7 us (30%)
  blocking collectives  82.3 us (27%)
  local copies, waits for them, and re-layouts  41.8 us (14%)
  matrix products  36.6 us (12%)
  other arithmetic  19.8 us (7%)
  starting transfers between devices  14.9 us (5%)
  between operations  14.1 us (5%)
    reduce_scatter x1, waiting for transfers between devices, local(): lax.psum_scatter(both, 'seq', scatter_dimension=0, tiled=True)  90.7 us
    psum x1, blocking collectives, local(): down_total, back_total = lax.psum((down_part, back_part), 'grp')  82.3 us
    all_to_all x1, starting transfers between devices, local(): out = lax.all_to_all(mixed, 'seq', split_axis=0, concat_axis=0, tiled=True)  14.8 us
    mul x1, local copies, waits for them, and re-layouts, local(): lb[:, :, None, :] * block_slot[:, None, :, None]  12.3 us
    mul x1, local copies, waits for them, and re-layouts, local(): ld[:, :, None, :] * block_slot[:, None, :, None]  12.3 us
    concatenate x1, other arithmetic, local(): jnp.concatenate([down_dense.reshape(trials, rank, depth), up_dense.reshap...  9.3 us
    dot_general x1, matrix products, local(): part = jnp.dot(x, w, preferred_element_type=jnp.float32)  8.85 us
    mul x1, other arithmetic, local(): lb[:, :, None, :] * block_slot[:, None, :, None]  7.08 us
  transfers between devices with their start and end apart: 3, of which 1 were waited for; matrix products, arithmetic and copies ran while one was open for 29% of the time, Pallas kernels for 0%

profile of v1, /device:TPU:1, one launch (start us, length us, event | category | flops | bytes accessed | tf_op | source)
XLA Modules:
  0.0 300.2 jit_solution(15265620093729976483)
XLA Ops:
  7.2 0.0 copy-start
  7.2 0.0 reduce-scatter.3.cloned.1.call-start
  7.2 1.5 copy-done
  8.8 8.8 %fusion.24 = f32[1024,2048]{1,0:T(8,128)} fusion(bf16[1024,1024]{1,0:T(8,128)(2,1)S(1)} %copy-done, bf16[1024,2048]{1,0:T(8,128)(2,1)} %param.11), kind=kOutput, calls=%fused_computation.30 | convolution fusion | flops 4294967296 | bytes 14680064 | tf_op jit(solution)/shard_map/dot_general | solution.py:27
  17.6 0.0 copy-start.3
  17.6 0.0 reduce-scatter.3.cloned.1.call-update
  17.6 0.0 reduce-scatter.5.cloned.1.call-start
  17.7 0.0 copy-start.1
  17.7 0.6 copy-done.3
  18.3 2.2 fusion.10
  20.5 2.6 convolution_bitcast_fusion
  23.0 0.0 copy-done.1
  23.1 5.7 %fusion.2 = bf16[32,1024,64]{1,0,2:T(8,128)(2,1)S(1)} fusion(bf16[32,1024,64]{1,2,0:T(8,128)(2,1)S(1)} %copy-done.1, s32[32]{0:T(128)S(1)} %bitcast.48), kind=kOutput, calls=%fused_computation.3 | convolution fusion | flops 134218752 | bytes 8388736 | tf_op jit(solution)/shard_map/bt,tfr->bfr/dot_general | solution.py:20
  28.7 0.0 copy-start.4
  28.7 3.6 %fusion.6 = f32[32,32,64]{2,1,0:T(8,128)} fusion(bf16[32,32,1024]{2,1,0:T(8,128)(2,1)S(1)} %bitcast.40, bf16[32,1024,64]{1,0,2:T(8,128)(2,1)S(1)} %fusion.2), kind=kOutput, calls=%fused_computation.10 | convolution fusion | flops 134217728 | bytes 6553600 | tf_op jit(solution)/shard_map/bpf,bfr->bpr/dot_general | solution.py:22
  32.3 0.0 copy-done.4
  32.3 0.2 fusion.16
  32.5 82.3 %all-reduce.2 = (bf16[32,32,64]{2,1,0:T(8,128)(2,1)S(1)}, bf16[32,32,64]{2,1,0:T(8,128)(2,1)}) all-reduce(f32[32,32,64]{2,1,0:T(8,128)} %fusion.6, f32[32,32,64]{2,1,0:T(8,128)} %convolution_bitcast_fusion), channel_id=1, replica_groups=mesh['grp'=8,'seq'=32] {'grp'}, use_global_device_ids=true, to_apply=%region_1.0 | all-reduce | flops 131072 | bytes 786432 | tf_op jit(solution)/shard_map/psum | solution.py:24
  114.9 7.1 %broadcast_multiply_fusion.1 = (bf16[32,32,32,64]{3,2,1,0:T(8,128)(2,1)}, bf16[32,32,32,64]{3,2,1,0:T(8,128)(2,1)}) fusion(bf16[32,32]{1,0:T(8,128)(2,1)S(1)} %fusion.16, bf16[32,32,64]{2,1,0:T(8,128)(2,1)} %get-tuple-element.4, bf16[32,32,64]{2,1,0:T(8,128)(2,1)S(1)} %get-tuple-element.3), kind=kLoop, calls=%fused_computation.6 | loop fusion | flops 4194304 | bytes 8652800 | tf_op jit(solution)/shard_map/mul | solution.py:29
  121.9 12.3 %mul.53 = bf16[1024,2048]{1,0:T(8,128)(2,1)} reshape(bf16[32,32,32,64]{3,2,1,0:T(8,128)(2,1)} %get-tuple-element.5) | data formatting | bytes 8388608 | tf_op jit(solution)/shard_map/mul | solution.py:29
  134.3 6.4 %copy.26 = bf16[2048,1024]{1,0:T(8,128)(2,1)} copy(bf16[2048,1024]{0,1:T(8,128)(2,1)} %bitcast.41) | data formatting | bytes 8388608 | tf_op jit(solution)/shard_map/nf,nq->qf/dot_general | solution.py:31
  140.7 12.3 %mul.56 = bf16[1024,2048]{1,0:T(8,128)(2,1)} reshape(bf16[32,32,32,64]{3,2,1,0:T(8,128)(2,1)} %get-tuple-element.6) | data formatting | bytes 8388608 | tf_op jit(solution)/shard_map/mul | solution.py:30
  153.0 6.4 %copy.27 = bf16[2048,1024]{1,0:T(8,128)(2,1)} copy(bf16[2048,1024]{0,1:T(8,128)(2,1)} %bitcast.42) | data formatting | bytes 8388608 | tf_op jit(solution)/shard_map/nq,no->qo/dot_general | solution.py:32
  159.4 0.0 copy-start.2
  159.4 5.0 %fusion.14 = f32[32,64,256]{2,1,0:T(8,128)} fusion(bf16[32,64,1024]{2,1,0:T(8,128)(2,1)} %bitcast.44, bf16[1024,256]{1,0:T(8,128)(2,1)} %param.8), kind=kOutput, calls=%fused_computation.18 | convolution fusion | flops 1073741824 | bytes 6815744 | tf_op jit(solution)/shard_map/nq,no->qo/dot_general | solution.py:32
  164.5 0.0 copy-done.2
  164.5 6.6 %fusion.4 = f32[32,64,1024]{2,1,0:T(8,128)} fusion(bf16[32,64,1024]{2,1,0:T(8,128)(2,1)S(1)} %bitcast.43, bf16[1024,1024]{1,0:T(8,128)(2,1)S(1)} %copy-done), kind=kOutput, calls=%fused_computation.7 | convolution fusion | flops 4294967296 | bytes 14680064 | tf_op jit(solution)/shard_map/nf,nq->qf/dot_general | solution.py:31
  171.1 9.3 %pad_maximum_fusion = f32[32,64,1280]{2,1,0:T(8,128)} fusion(f32[32,64,256]{2,1,0:T(8,128)} %fusion.14, f32[32,64,1024]{2,1,0:T(8,128)} %fusion.4), kind=kLoop, calls=%fused_computation | loop fusion | flops 2621440 | bytes 20971520 | tf_op jit(solution)/shard_map/concatenate | solution.py:33
  180.4 0.0 reduce-scatter.5.cloned.1.call-update
  180.4 1.8 convolution_multiply_fusion
  182.3 0.0 reduce-scatter.3.cloned.1.call-done
  182.3 2.4 fusion.9
  184.7 14.8 %all-to-all-start = ((bf16[32,32,256]{2,1,0:T(8,128)(2,1)}), bf16[32,32,256]{2,1,0:T(8,128)(2,1)S(1)}, u32[]{:S(2)}, u32[]{:S(2)}) async-start(bf16[32,32,256]{2,1,0:T(8,128)(2,1)} %bitcast.5), calls=%async_computation.1 | async-start | bytes 1048576 | tf_op jit(solution)/shard_map/all_to_all | solution.py:37
  199.5 90.7 %reduce-scatter.5.cloned.1.call-done = f32[1,64,1280]{2,1,0:T(8,128)} async-done(((f32[32,64,1280]{2,1,0:T(8,128)}), f32[1,64,1280]{2,1,0:T(8,128)}) %reduce-scatter.5.cloned.1.call-update) | async-done | bytes 327696 | tf_op jit(solution)/shard_map/reduce_scatter | solution.py:34
  290.2 1.0 broadcast_multiply_fusion.2
  291.2 0.6 slice.9
  291.9 0.7 slice_bitcast_fusion
  292.6 0.0 all-to-all-done
  292.6 0.8 copy.45
Async XLA Ops:
  7.2 1.6 copy-start
  7.2 175.1 %reduce-scatter.3.cloned.1.call-start = ((), (), s32[]{:S(2)}) async-start(), calls=%async_computation.3 | async-start | bytes 9437184 | tf_op jit(solution)/shard_map/reduce_scatter | solution.py:28
  17.6 0.7 copy-start.3
  17.6 272.6 %reduce-scatter.5.cloned.1.call-start = ((), (), s32[]{:S(2)}) async-start(), calls=%async_computation.4 | async-start | bytes 10813440 | tf_op jit(solution)/shard_map/reduce_scatter | solution.py:34
  17.7 5.4 %copy-start.1 = (bf16[32,1024,64]{1,2,0:T(8,128)(2,1)S(1)}, bf16[32,1024,64]{1,2,0:T(8,128)(2,1)}, u32[]{:S(2)}) copy-start(bf16[32,1024,64]{1,2,0:T(8,128)(2,1)} %param.12) | copy-start | bytes 12582916
  28.7 3.6 %copy-start.4 = (s32[32]{0:T(128)S(1)}, s32[32]{0:T(128)}, u32[]{:S(2)}) copy-start(s32[32]{0:T(128)} %param.10) | copy-start | bytes 388
  159.4 5.0 %copy-start.2 = (bf16[2048,1024]{1,0:T(8,128)(2,1)S(1)}, bf16[2048,1024]{1,0:T(8,128)(2,1)}, u32[]{:S(2)}) copy-start(bf16[2048,1024]{1,0:T(8,128)(2,1)} %copy.26) | copy-start | bytes 12582916
  184.7 107.9 %all-to-all-start = ((bf16[32,32,256]{2,1,0:T(8,128)(2,1)}), bf16[32,32,256]{2,1,0:T(8,128)(2,1)S(1)}, u32[]{:S(2)}, u32[]{:S(2)}) async-start(bf16[32,32,256]{2,1,0:T(8,128)(2,1)} %bitcast.5), calls=%async_computation.1 | async-start | bytes 1048576 | tf_op jit(solution)/shard_map/all_to_all | solution.py:37
Sparse Core Ops, SparseCore 0:
  17.8 118.4 reduce-scatter.2
  180.5 109.6 reduce-scatter.4

commit v2 on v1

v2 whole, which is shorter than its diff:
```python
import jax
import jax.numpy as jnp
from jax import lax
from jax.experimental import pallas as pl
from jax.experimental.pallas import tpu as pltpu
from jax.sharding import PartitionSpec as P

ADAPTER_SCALE = 2.0
MESH = pl.DeviceIdType.MESH
F32, BF16 = jnp.float32, jnp.bfloat16
NT = (((1,), (1,)), ((), ()))
TN = (((0,), (0,)), ((), ()))
Z, Y, X, C = 8, 4, 4, 2
SEQ = Y * X * C
CHUNKS = 4


def loop(n, body):
    lax.fori_loop(0, n, lambda i, c: (body(i), c)[1], 0)


def kernel(
    meta, x_h, g_h, w_h, d_h, u_h, out_h, ga_o, gb_o,
    xv, gv, wv, dv, uv, sbuf, rbuf, lp, lsb, lrb, lall, s1, r1, sg, ra, rb, ta, tb, ra3, rb3, fin, branch, mix,
    ld_sem, zs, zr, ls, lr, ags, agr, s1s, s1r, ras, rar, rbs, rbr, tas, tar, tbs, tbr, os, orr, loc,
):
    zi, si = lax.axis_index("grp"), lax.axis_index("seq")
    ci, xi, yi = si % C, (si // C) % X, si // (C * X)
    blocks, blk, depth = xv.shape
    cols = gv.shape[2]
    rank = dv.shape[1]
    half = rank // 2
    per = blocks // CHUNKS
    wide = depth + cols

    def seq_at(y, x, c):
        return (y * X + x) * C + c

    barrier = pltpu.get_barrier_semaphore()
    loop(SEQ - 1, lambda o: pl.semaphore_signal(barrier, inc=1, device_id={"seq": (si + o + 1) % SEQ}, device_id_type=MESH))
    loop(Z - 1, lambda o: pl.semaphore_signal(barrier, inc=1, device_id={"grp": (zi + o + 1) % Z}, device_id_type=MESH))

    def w_copy(r):
        at = pl.multiple_of(((zi + r) % Z) * cols, cols)
        return pltpu.make_async_copy(w_h.at[:, pl.ds(at, cols)], wv.at[r], ld_sem.at[r])

    x_copy = pltpu.make_async_copy(x_h, xv, ld_sem.at[8])
    g_copy = pltpu.make_async_copy(g_h, gv, ld_sem.at[9])
    d_copy = pltpu.make_async_copy(d_h, dv, ld_sem.at[10])
    u_copy = pltpu.make_async_copy(u_h, uv, ld_sem.at[11])
    x_copy.start()
    w_copy(4).start()
    d_copy.start()
    g_copy.start()
    u_copy.start()
    for r in (3, 5, 2, 6, 1, 7, 0):
        w_copy(r).start()

    def rows_of(q):
        return ((yi + q + 1) % Y) * per

    def own(q, r):
        rows = xv[pl.ds(rows_of(q), per)].reshape(per * blk, depth)
        return jnp.dot(rows, wv[r], preferred_element_type=F32)

    def z_copy(dr, q, d):
        return pltpu.make_async_remote_copy(
            src_ref=sbuf.at[dr, q, d - 1], dst_ref=rbuf.at[dr, q, d - 1],
            send_sem=zs.at[dr, q, d - 1], recv_sem=zr.at[dr, q, d - 1],
            device_id={"grp": (zi + 1 - 2 * dr + Z) % Z}, device_id_type=MESH,
        )

    def event(dr, q, d, first):
        v = own(q, ((1 - 2 * dr) * d + Z) % Z)
        if not first:
            z_copy(dr, q, d + 1).wait_recv()
            v = v + rbuf[dr, q, d].astype(F32)
        sbuf[dr, q, d - 1] = v.astype(BF16)
        z_copy(dr, q, d).start()

    def l_copy(dr, h, d):
        return pltpu.make_async_remote_copy(
            src_ref=lsb.at[dr, h, d - 1], dst_ref=lrb.at[dr, h, d - 1],
            send_sem=ls.at[dr, h, d - 1], recv_sem=lr.at[dr, h, d - 1],
            device_id={"grp": (zi + 1 - 2 * dr + Z) % Z}, device_id_type=MESH,
        )

    def l_rows(r, h):
        return pl.ds(((zi + r) % Z) * 4 + 2 * h, 2)

    def l_step(d):
        for h in range(2):
            for dr in range(2):
                length = 4 if h == dr else 3
                if d > length:
                    continue
                v = lp[l_rows(((1 - 2 * dr) * d + Z) % Z, h)]
                if d < length:
                    l_copy(dr, h, d + 1).wait_recv()
                    v = v + lrb[dr, h, d]
                lsb[dr, h, d - 1] = v
                l_copy(dr, h, d).start()

    def gather_copy(o, source):
        at = pl.ds(source * 4, 4)
        return pltpu.make_async_remote_copy(
            src_ref=lall.at[at], dst_ref=lall.at[at], send_sem=ags.at[o - 1], recv_sem=agr.at[o - 1],
            device_id={"grp": (zi + o) % Z}, device_id_type=MESH,
        )

    x_copy.wait()
    w_copy(4).wait()
    pl.semaphore_wait(barrier, SEQ - 1 + Z - 1)

    loop(4, lambda i: event(i % 2, 2 * (i % 2) + i // 2, 4, True))

    d_copy.wait()
    g_copy.wait()
    u_copy.wait()

    def rank_block(b):
        t = meta[0, b]
        down = lax.dot_general(xv[b], dv[t], NT, preferred_element_type=F32)
        back = lax.dot_general(gv[b], uv[t], NT, preferred_element_type=F32)
        lp[b] = jnp.concatenate([down, back], axis=1)

    loop(blocks, rank_block)
    l_step(4)
    for r in (3, 5):
        w_copy(r).wait()
    loop(2, lambda i: event(i % 2, 2 * (1 - i % 2) + i // 2, 3, True))
    l_step(3)
    loop(2, lambda i: event(i % 2, 2 * (1 - i % 2) + 1, 3, True))
    l_step(2)
    loop(2, lambda i: event(i % 2, 2 * (i % 2) + i // 2, 3, False))
    l_step(1)
    loop(2, lambda i: event(i % 2, 2 * (i % 2) + 1, 3, False))
    for h in range(2):
        for dr in range(2):
            l_copy(dr, h, 1).wait_recv()
        v = lp[l_rows(0, h)] + lrb[0, h, 0] + lrb[1, h, 0]
        lall[l_rows(0, h)] = v.astype(BF16)
    for o in (4, 3, 5, 2, 6, 1, 7):
        gather_copy(o, zi).start()

    for r in (2, 6):
        w_copy(r).wait()
    loop(8, lambda i: event(i % 2, i // 2, 2, False))

    for o in range(1, Z):
        gather_copy(o, (zi - o + Z) % Z).wait_recv()

    def grads(k):
        b1, b2 = meta[1, k], meta[2, k]
        m1, m2 = meta[3, k].astype(F32), meta[4, k].astype(F32)
        rows = jnp.concatenate([lall[b1].astype(F32) * m1, lall[b2].astype(F32) * m2], axis=0).astype(BF16)
        xs = jnp.concatenate([xv[b1], xv[b2]], axis=0)
        gs = jnp.concatenate([gv[b1], gv[b2]], axis=0)
        return (
            lax.dot_general(rows[:, rank:], xs, TN, preferred_element_type=F32),
            lax.dot_general(rows[:, :rank], gs, TN, preferred_element_type=F32),
        )

    def pair_copy(j):
        return pltpu.make_async_remote_copy(
            src_ref=s1.at[j], dst_ref=r1.at[j], send_sem=s1s.at[j], recv_sem=s1r.at[j],
            device_id={"seq": seq_at(yi, xi, 1 - ci)}, device_id_type=MESH,
        )

    def for_sibling(i):
        j = X * Y - 1 - i
        ga, gb = grads(seq_at((yi + j // X) % Y, (xi + j % X) % X, 1 - ci))
        s1[j, :, :depth] = ga.astype(BF16)
        s1[j, :, depth:] = gb.astype(BF16)
        pair_copy(j).start()

    def a_copy(oy, ox):
        return pltpu.make_async_remote_copy(
            src_ref=sg.at[oy * X + ox, 0], dst_ref=ra.at[ox - 1, oy], send_sem=ras.at[ox - 1, oy], recv_sem=rar.at[ox - 1, oy],
            device_id={"seq": seq_at(yi, (xi + ox) % X, ci)}, device_id_type=MESH,
        )

    def b_copy(oy, ox):
        return pltpu.make_async_remote_copy(
            src_ref=sg.at[oy * X + ox, 1], dst_ref=rb.at[oy - 1, ox], send_sem=rbs.at[oy - 1, ox], recv_sem=rbr.at[oy - 1, ox],
            device_id={"seq": seq_at((yi + oy) % Y, xi, ci)}, device_id_type=MESH,
        )

    def a_last(o):
        return pltpu.make_async_remote_copy(
            src_ref=ta.at[o - 1], dst_ref=ra3.at[o - 1], send_sem=tas.at[o - 1], recv_sem=tar.at[o - 1],
            device_id={"seq": seq_at((yi + o) % Y, xi, ci)}, device_id_type=MESH,
        )

    def b_last(o):
        return pltpu.make_async_remote_copy(
            src_ref=tb.at[o - 1], dst_ref=rb3.at[o - 1], send_sem=tbs.at[o - 1], recv_sem=tbr.at[o - 1],
            device_id={"seq": seq_at(yi, (xi + o) % X, ci)}, device_id_type=MESH,
        )

    def for_pair(i):
        j = X * Y - 1 - i
        oy, ox = j // X, j % X
        ga, gb = grads(seq_at((yi + oy) % Y, (xi + ox) % X, ci))
        pair_copy(j).wait_recv()
        ga = (ga + r1[j, :, :depth].astype(F32)).astype(BF16)
        gb = (gb + r1[j, :, depth:].astype(F32)).astype(BF16)
        for h in range(2):
            sg[j, h, :, :depth] = ga[h * half : (h + 1) * half]
            sg[j, h, :, depth:] = gb[h * half : (h + 1) * half]

        @pl.when(ox > 0)
        def _():
            a_copy(oy, ox).start()

        @pl.when(oy > 0)
        def _():
            b_copy(oy, ox).start()

    loop(X * Y, for_sibling)
    loop(X * Y, for_pair)

    for r in (1, 7):
        w_copy(r).wait()
    loop(8, lambda i: event(i % 2, i // 2, 1, False))

    def branch_block(b):
        v = jnp.dot(lall[b][:, :rank], uv[meta[0, b]], preferred_element_type=F32)
        branch[b] = ADAPTER_SCALE * v

    loop(blocks, branch_block)

    for o in (2, 1, 3, 0):
        for p in range(1, 4):
            a_copy(o, p).wait_recv()
            b_copy(p, o).wait_recv()
        va, vb = sg[o * X, 0].astype(F32), sg[o, 1].astype(F32)
        for p in range(3):
            va = va + ra[p, o].astype(F32)
            vb = vb + rb[p, o].astype(F32)
        if o == 0:
            fin[0], fin[1] = va, vb
        else:
            ta[o - 1], tb[o - 1] = va.astype(BF16), vb.astype(BF16)
            a_last(o).start()
            b_last(o).start()

    def out_copy(q, i):
        target = seq_at((yi + q + 1) % Y, (xi + i // 2) % X, (ci + i) % C)
        return pltpu.make_async_remote_copy(
            src_ref=mix.at[target], dst_ref=out_h.at[si], send_sem=os.at[q, i], recv_sem=orr.at[q, i],
            device_id={"seq": target}, device_id_type=MESH,
        )

    def out_arrival(q, i):
        source = seq_at((yi + 2 * Y - q - 1) % Y, (xi + X - i // 2) % X, (ci + i) % C)
        return pltpu.make_async_remote_copy(
            src_ref=mix.at[source], dst_ref=out_h.at[source], send_sem=os.at[q, i], recv_sem=orr.at[q, i],
            device_id={"seq": source}, device_id_type=MESH,
        )

    self_copy = pltpu.make_async_copy(mix.at[si], out_h.at[si], loc)
    w_copy(0).wait()

    def finish(q):
        v = own(q, 0)
        for dr in range(2):
            z_copy(dr, q, 1).wait_recv()
        v = v + rbuf[0, q, 0].astype(F32) + rbuf[1, q, 0].astype(F32)
        at = pl.ds(rows_of(q), per)
        mix[at] = (v.reshape(per, blk, cols) + branch[at]).astype(BF16)

        def send(i):
            @pl.when(q * per + i != (CHUNKS - 1) * per)
            def _():
                out_copy(q, i).start()

        loop(per, send)

    loop(CHUNKS, finish)
    self_copy.start()

    for o in range(1, 4):
        a_last(o).wait_recv()
        b_last(o).wait_recv()
    for h, last in ((0, ra3), (1, rb3)):
        v = fin[h]
        for p in range(3):
            v = v + last[p].astype(F32)
        v = ADAPTER_SCALE * v
        ga_o[0, h * half : (h + 1) * half] = v[:, :depth]
        gb_o[0, h * half : (h + 1) * half] = v[:, depth:]

    def out_wait(n):
        @pl.when(n != (CHUNKS - 1) * per)
        def _():
            out_arrival(n // per, n % per).wait_recv()
            out_copy(n // per, n % per).wait_send()

    loop(blocks, out_wait)
    self_copy.wait()

    loop(4, lambda i: z_copy(i % 2, 2 * (i % 2) + i // 2, 4).wait_send())
    loop(24, lambda i: z_copy(i % 2, (i // 2) % 4, i // 8 + 1).wait_send())
    for dr in range(2):
        for h in range(2):
            for d in range(1, 5 if h == dr else 4):
                l_copy(dr, h, d).wait_send()
    for o in range(1, Z):
        gather_copy(o, zi).wait_send()
    loop(X * Y, lambda j: pair_copy(j).wait_send())
    for o in range(4):
        for p in range(1, 4):
            a_copy(o, p).wait_send()
            b_copy(p, o).wait_send()
    for o in range(1, 4):
        a_last(o).wait_send()
        b_last(o).wait_send()


def tables(trial_per_block, trial_slot_index):
    blocks = trial_per_block.shape[0]
    trials = trial_slot_index.shape[0]
    trial = trial_per_block[:, 0]
    numbers = jnp.arange(trials, dtype=jnp.int32)
    slot = jnp.sum(jnp.where(trial[:, None] == numbers[None, :], trial_slot_index[None, :], 0), axis=1)
    here = slot[None, :] == numbers[:, None]
    block = jnp.arange(blocks, dtype=jnp.int32)[None, :]
    first = jnp.min(jnp.where(here, block, blocks), axis=1)
    last = jnp.max(jnp.where(here, block, -1), axis=1)
    return jnp.stack([
        trial, jnp.minimum(first, blocks - 1), jnp.maximum(last, 0),
        (last >= 0).astype(jnp.int32), (last > first).astype(jnp.int32),
    ])


def local(x, g, trial_per_block, trial_slot_index, w, down, up):
    blocks = trial_per_block.shape[0]
    trials, depth, rank = down.shape
    cols = up.shape[2]
    blk = x.shape[0] // blocks
    half, wide = rank // 2, depth + cols
    chunk = x.shape[0] // CHUNKS
    hbm = pl.BlockSpec(memory_space=pl.ANY)
    vmem = pl.BlockSpec(memory_space=pltpu.VMEM)
    dma = pltpu.SemaphoreType.DMA
    out, ga, gb = pl.pallas_call(
        kernel,
        out_shape=(
            jax.ShapeDtypeStruct((SEQ, blk, cols), BF16),
            jax.ShapeDtypeStruct((1, rank, depth), F32),
            jax.ShapeDtypeStruct((1, rank, cols), F32),
        ),
        in_specs=[pl.BlockSpec(memory_space=pltpu.SMEM)] + [hbm] * 5,
        out_specs=(hbm, vmem, vmem),
        scratch_shapes=[
            pltpu.VMEM((blocks, blk, depth), BF16),
            pltpu.VMEM((blocks, blk, cols), BF16),
            pltpu.VMEM((Z, depth, cols), BF16),
            pltpu.VMEM((trials, rank, depth), BF16),
            pltpu.VMEM((trials, rank, cols), BF16),
            pltpu.VMEM((2, CHUNKS, 4, chunk, cols), BF16),
            pltpu.VMEM((2, CHUNKS, 4, chunk, cols), BF16),
            pltpu.VMEM((blocks, blk, 2 * rank), F32),
            pltpu.VMEM((2, 2, 4, 2, blk, 2 * rank), F32),
            pltpu.VMEM((2, 2, 4, 2, blk, 2 * rank), F32),
            pltpu.VMEM((blocks, blk, 2 * rank), BF16),
            pltpu.VMEM((X * Y, rank, wide), BF16),
            pltpu.VMEM((X * Y, rank, wide), BF16),
            pltpu.VMEM((X * Y, 2, half, wide), BF16),
            pltpu.VMEM((3, 4, half, wide), BF16),
            pltpu.VMEM((3, 4, half, wide), BF16),
            pltpu.VMEM((3, half, wide), BF16),
            pltpu.VMEM((3, half, wide), BF16),
            pltpu.VMEM((3, half, wide), BF16),
            pltpu.VMEM((3, half, wide), BF16),
            pltpu.VMEM((2, half, wide), F32),
            pltpu.VMEM((blocks, blk, cols), F32),
            pltpu.VMEM((blocks, blk, cols), BF16),
            dma((12,)),
            dma((2, CHUNKS, 4)), dma((2, CHUNKS, 4)),
            dma((2, 2, 4)), dma((2, 2, 4)),
            dma((Z - 1,)), dma((Z - 1,)),
            dma((X * Y,)), dma((X * Y,)),
            dma((3, 4)), dma((3, 4)), dma((3, 4)), dma((3, 4)),
            dma((3,)), dma((3,)), dma((3,)), dma((3,)),
            dma((CHUNKS, blocks // CHUNKS)), dma((CHUNKS, blocks // CHUNKS)),
            dma,
        ],
        compiler_params=pltpu.CompilerParams(collective_id=0, has_side_effects=True, vmem_limit_bytes=56 * 2**20),
    )(
        tables(trial_per_block, trial_slot_index),
        x.reshape(blocks, blk, depth), g.reshape(blocks, blk, cols), w, jnp.transpose(down, (0, 2, 1)), up,
    )
    return out.reshape(x.shape[0], cols), jnp.transpose(ga, (0, 2, 1)), gb


def solution(mesh):
    in_specs = (
        P("seq", "grp"),
        P("seq", "grp"),
        P("seq", None),
        P(),
        P("grp", None),
        P(None, "grp", None),
        P(None, None, "grp"),
    )
    out_specs = (P("seq", "grp"), P("seq", "grp", None), P("seq", None, "grp"))
    return jax.shard_map(local, mesh=mesh, in_specs=in_specs, out_specs=out_specs, check_vma=False)
```

time: 301 us -> 89.9 us (0.30)
  waiting for transfers between devices: 90.7 us -> 0 us
  blocking collectives: 82.3 us -> 0 us
  Pallas kernels: 0 us -> 81.7 us
  matrix products: 36.6 us -> 0 us
  local copies, waits for them, and re-layouts: 41.8 us -> 6.27 us
  other arithmetic: 19.8 us -> 0.98 us
  starting transfers between devices: 14.9 us -> 0 us
  between operations: 14.1 us -> 0.66 us
    reduce_scatter x2 -> x0, waiting for transfers between devices: 90.7 us -> none  [the longest x1 90.7 us: local(): lax.psum_scatter(both, 'seq', scatter_dimension=0, tiled=True)]
    psum x1 -> x0, blocking collectives: 82.3 us -> none  [local(): down_total, back_total = lax.psum((down_part, back_part), 'grp')]
    pallas_call x0 -> x1, Pallas kernels: none -> 81.7 us  [local(): pl.pallas_call(kernel, out_shape=(jax.ShapeDtypeStruct((SEQ, blk, cols),...]
    dot_general x9 -> x0, matrix products: 36.6 us -> none  [the longest x1 8.85 us: local(): part = jnp.dot(x, w, preferred_element_type=jnp.float32)]
    mul x2 -> x0, local copies, waits for them, and re-layouts: 24.7 us -> none  [the longest x1 12.3 us: local(): lb[:, :, None, :] * block_slot[:, None, :, None]]
    all_to_all x1 -> x0, starting transfers between devices: 14.8 us -> none  [local(): out = lax.all_to_all(mixed, 'seq', split_axis=0, concat_axis=0, tiled=True)]
    dot_general x2 -> x0, local copies, waits for them, and re-layouts: 12.8 us -> none  [the longest x1 6.41 us: local(): jnp.einsum('nf,nq->qf', x, lb_all, preferred_element_type=jnp.float32)]
    concatenate x1 -> x0, other arithmetic: 9.3 us -> none  [local(): jnp.concatenate([down_dense.reshape(trials, rank, depth), up_dense.reshap...]
  transfers between devices with their start and end apart: 3 -> 0, of which waited for: 1 -> 0; matrix products, arithmetic and copies ran while one was open for 29% -> 0% of each run, Pallas kernels for 0% -> 0%
where the time goes in v2:
time: 89.9 us; the launch traced here: 89.6 us
  Pallas kernels  81.7 us (91%)
  local copies, waits for them, and re-layouts  6.27 us (7%)
  other arithmetic  0.98 us (1%)
    pallas_call x1, Pallas kernels, local(): pl.pallas_call(kernel, out_shape=(jax.ShapeDtypeStruct((SEQ, blk, cols),...  81.7 us
    unnamed x3, local copies, waits for them, and re-layouts  5.01 us

profile of v2, /device:TPU:1, one launch (start us, length us, event | category | flops | bytes accessed | tf_op | source)
XLA Modules:
  0.0 89.6 jit_solution(11166030070987634977)
XLA Ops:
  0.6 0.9 select_reduce_fusion.2
  1.5 0.1 select_reduce_fusion
  1.6 1.3 %stack.2.meta = s32[5,32]{1,0:T(8,128)} concatenate(s32[1,32]{1,0:T(1,128)} %bitcast.21, s32[1,32]{1,0:T(1,128)S(1)} %get-tuple-element.14, s32[1,32]{1,0:T(1,128)S(1)} %get-tuple-element.13, s32[1,32]{1,0:T(1,128)S(1)} %get-tuple-element.12, s32[1,32]{1,0:T(1,128)S(1)} %get-tuple-element.11), dimensions={0} | concatenate | bytes 1280 | tf_op jit(solution)/shard_map/stack | solution.py:331
  2.9 81.7 %shard_map.94 = (bf16[32,32,256]{2,1,0:T(8,128)(2,1)}, f32[1,64,1024]{2,1,0:T(8,128)}, f32[1,64,256]{2,1,0:T(8,128)}) custom-call(s32[5,32]{1,0:T(8,128)} %stack.2.meta, bf16[32,32,1024]{2,1,0:T(8,128)(2,1)} %bitcast.16, bf16[32,32,256]{2,1,0:T(8,128)(2,1)} %bitcast.17, bf16[1024,2048]{1,0:T(8,128)(2,1)} %w_h.1, bf16[32,64,1024]{2,1,0:T(8,128)(2,1)} %bitcast.15, ...), custom_call_target="tpu_custom_call" | custom-call | tf_op jit(solution)/shard_map/pallas_call | solution.py:347
  84.6 1.9 %copy.13 = bf16[1024,256]{1,0:T(8,128)(2,1)} copy(bf16[1024,256]{1,0:T(8,128)(2,1)} %bitcast.18) | data formatting | bytes 1048576
  86.5 1.7 %copy.14 = f32[1,1024,64]{1,2,0:T(8,128)} copy(f32[1,1024,64]{1,2,0:T(8,128)} %bitcast.19) | data formatting | bytes 524288
  88.1 1.5 %copy.15 = f32[1,64,256]{2,1,0:T(8,128)} copy(f32[1,64,256]{2,1,0:T(8,128)} %get-tuple-element.20) | data formatting | bytes 131072
  (2 shorter events, 0.0 us)

commit v3 on v2

v3 whole, which is shorter than its diff:
```python
import jax
import jax.numpy as jnp
from jax import lax
from jax.experimental import pallas as pl
from jax.experimental.pallas import tpu as pltpu
from jax.sharding import PartitionSpec as P

ADAPTER_SCALE = 2.0
MESH = pl.DeviceIdType.MESH
F32, BF16 = jnp.float32, jnp.bfloat16
RANK_SENT = BF16
NT = (((1,), (1,)), ((), ()))
TN = (((0,), (0,)), ((), ()))
Z, Y, X, C = 8, 4, 4, 2
SEQ = Y * X * C
CHUNKS = 4


ORDER = (
    (2, 2), (0, 2), (2, 0), (1, 2), (3, 2), (2, 1), (2, 3), (1, 1),
    (1, 3), (3, 1), (3, 3), (0, 1), (0, 3), (1, 0), (3, 0), (0, 0),
)


def loop(n, body, unroll=1):
    lax.fori_loop(0, n, lambda i, c: (body(i), c)[1], 0, unroll=unroll)


def kernel(
    trial, slot, trial_row, x_h, g_h, w_h, d_h, u_h, out_h, ga_o, gb_o,
    tab_v, tab, xv, gv, wv, dv, uv, sbuf, rbuf, lp, lsb, lrb, lall, s1, r1, sg, rf, ra, ta, tb, ra3, rb3, fin, branch, mix,
    ld_sem, zs, zr, ls, lr, ags, agr, s1s, s1r, rfs, rfr, ras, rar, tas, tar, tbs, tbr, os, orr, loc,
):
    zi, si = lax.axis_index("grp"), lax.axis_index("seq")
    ci, xi, yi = si % C, (si // C) % X, si // (C * X)
    blocks, blk, depth = xv.shape
    cols = gv.shape[2]
    rank = dv.shape[1]
    half = rank // 2
    per = blocks // CHUNKS
    wide = depth + cols

    def seq_at(y, x, c):
        return (y * X + x) * C + c

    barrier = pltpu.get_barrier_semaphore()
    loop(SEQ - 1, lambda o: pl.semaphore_signal(barrier, inc=1, device_id={"seq": (si + o + 1) % SEQ}, device_id_type=MESH))
    loop(Z - 1, lambda o: pl.semaphore_signal(barrier, inc=1, device_id={"grp": (zi + o + 1) % Z}, device_id_type=MESH))

    def w_copy(r):
        at = pl.multiple_of(((zi + r) % Z) * cols, cols)
        return pltpu.make_async_copy(w_h.at[:, pl.ds(at, cols)], wv.at[r], ld_sem.at[r])

    x_copy = pltpu.make_async_copy(x_h, xv, ld_sem.at[8])
    g_copy = pltpu.make_async_copy(g_h, gv, ld_sem.at[9])
    d_copy = pltpu.make_async_copy(d_h, dv, ld_sem.at[10])
    u_copy = pltpu.make_async_copy(u_h, uv, ld_sem.at[11])
    x_copy.start()
    w_copy(4).start()
    d_copy.start()
    g_copy.start()
    u_copy.start()
    for r in (3, 5, 2, 6, 1, 7, 0):
        w_copy(r).start()

    def rows_of(q):
        return ((yi + q + 1) % Y) * per

    def own(q, r):
        rows = xv[pl.ds(rows_of(q), per)].reshape(per * blk, depth)
        return jnp.dot(rows, wv[r], preferred_element_type=F32)

    def z_copy(dr, q, d):
        return pltpu.make_async_remote_copy(
            src_ref=sbuf.at[dr, q, d - 1], dst_ref=rbuf.at[dr, q, d - 1],
            send_sem=zs.at[dr, q, d - 1], recv_sem=zr.at[dr, q, d - 1],
            device_id={"grp": (zi + 1 - 2 * dr + Z) % Z}, device_id_type=MESH,
        )

    def event(dr, q, d, first):
        v = own(q, ((1 - 2 * dr) * d + Z) % Z)
        if not first:
            z_copy(dr, q, d + 1).wait_recv()
            v = v + rbuf[dr, q, d].astype(F32)
        sbuf[dr, q, d - 1] = v.astype(BF16)
        z_copy(dr, q, d).start()

    def l_copy(o):
        return pltpu.make_async_remote_copy(
            src_ref=lsb.at[pl.ds(((zi + o) % Z) * 4, 4)], dst_ref=lrb.at[o - 1], send_sem=ls.at[o - 1], recv_sem=lr.at[o - 1],
            device_id={"grp": (zi + o) % Z}, device_id_type=MESH,
        )

    def gather_copy(o, source):
        at = pl.ds(source * 4, 4)
        return pltpu.make_async_remote_copy(
            src_ref=lall.at[at], dst_ref=lall.at[at], send_sem=ags.at[o - 1], recv_sem=agr.at[o - 1],
            device_id={"grp": (zi + o) % Z}, device_id_type=MESH,
        )

    count = slot.shape[0]
    slot_row = jnp.zeros((1, blocks), jnp.int32)
    for t in range(count):
        slot_row = jnp.where(trial_row[...] == t, slot[t], slot_row)
    here = jnp.broadcast_to(slot_row, (count, blocks)) == lax.broadcasted_iota(jnp.int32, (count, blocks), 0)
    number = lax.broadcasted_iota(jnp.int32, (count, blocks), 1)
    first = jnp.min(jnp.where(here, number, blocks), axis=1, keepdims=True)
    last = jnp.max(jnp.where(here, number, -1), axis=1, keepdims=True)
    lane = lax.broadcasted_iota(jnp.int32, tab_v.shape, 1)
    row = jnp.where(lane == 0, jnp.minimum(first, blocks - 1), jnp.maximum(last, 0))
    row = jnp.where(lane == 2, (last >= 0).astype(jnp.int32), row)
    tab_v[...] = jnp.where(lane == 3, (last > first).astype(jnp.int32), row)
    tab_copy = pltpu.make_async_copy(tab_v, tab, ld_sem.at[12])
    tab_copy.start()

    x_copy.wait()
    w_copy(4).wait()
    pl.semaphore_wait(barrier, SEQ - 1 + Z - 1)

    loop(4, lambda i: event(i % 2, 2 * (i % 2) + i // 2, 4, True), 2)

    d_copy.wait()
    g_copy.wait()
    u_copy.wait()

    def rank_block(b):
        t = trial[b]
        down = lax.dot_general(xv[b], dv[t], NT, preferred_element_type=F32)
        back = lax.dot_general(gv[b], uv[t], NT, preferred_element_type=F32)
        v = jnp.concatenate([down, back], axis=1)
        lp[b] = v
        lsb[b] = v.astype(lsb.dtype)

    loop(blocks, rank_block, 8)
    for o in (4, 3, 5, 2, 6, 1, 7):
        l_copy(o).start()
    for r in (3, 5):
        w_copy(r).wait()
    loop(4, lambda i: event(i % 2, 2 * (1 - i % 2) + i // 2, 3, True), 2)
    mine = pl.ds(zi * 4, 4)
    v = lp[mine]
    for o in range(1, Z):
        l_copy(o).wait_recv()
        v = v + lrb[o - 1].astype(F32)
    lall[mine] = v.astype(BF16)
    for o in (4, 3, 5, 2, 6, 1, 7):
        gather_copy(o, zi).start()
    loop(4, lambda i: event(i % 2, 2 * (i % 2) + i // 2, 3, False), 2)

    for o in range(1, Z):
        gather_copy(o, (zi - o + Z) % Z).wait_recv()

    def grads(k):
        b1, b2 = tab[k, 0], tab[k, 1]
        m1, m2 = tab[k, 2].astype(F32), tab[k, 3].astype(F32)
        rows = jnp.concatenate([lall[b1].astype(F32) * m1, lall[b2].astype(F32) * m2], axis=0).astype(BF16)
        xs = jnp.concatenate([xv[b1], xv[b2]], axis=0)
        gs = jnp.concatenate([gv[b1], gv[b2]], axis=0)
        return (
            lax.dot_general(rows[:, rank:], xs, TN, preferred_element_type=F32),
            lax.dot_general(rows[:, :rank], gs, TN, preferred_element_type=F32),
        )

    def pair_copy(j):
        return pltpu.make_async_remote_copy(
            src_ref=s1.at[j], dst_ref=r1.at[j], send_sem=s1s.at[j], recv_sem=s1r.at[j],
            device_id={"seq": seq_at(yi, xi, 1 - ci)}, device_id_type=MESH,
        )

    def for_sibling(i):
        oy, ox = ORDER[i]
        j = oy * X + ox
        ga, gb = grads(seq_at((yi + oy) % Y, (xi + ox) % X, 1 - ci))
        s1[j, :, :depth] = ga.astype(BF16)
        s1[j, :, depth:] = gb.astype(BF16)
        pair_copy(j).start()

    def slot_of(h, p, o):
        return o * X + p if h == 0 else p * X + o

    def along(h, p):
        return {"seq": seq_at(yi, (xi + p) % X, ci) if h == 0 else seq_at((yi + p) % Y, xi, ci)}

    def far_copy(h, w, o):
        return pltpu.make_async_remote_copy(
            src_ref=sg.at[slot_of(h, 2, o), h, pl.ds(w * half // 2, half // 2)], dst_ref=rf.at[h, w, o],
            send_sem=rfs.at[h, w, o], recv_sem=rfr.at[h, w, o], device_id=along(h, 1 + 2 * w), device_id_type=MESH,
        )

    def near_copy(h, w, o):
        return pltpu.make_async_remote_copy(
            src_ref=sg.at[slot_of(h, 1 + 2 * w, o), h], dst_ref=ra.at[h, w, o],
            send_sem=ras.at[h, w, o], recv_sem=rar.at[h, w, o], device_id=along(h, 1 + 2 * w), device_id_type=MESH,
        )

    def a_last(o):
        return pltpu.make_async_remote_copy(
            src_ref=ta.at[o - 1], dst_ref=ra3.at[o - 1], send_sem=tas.at[o - 1], recv_sem=tar.at[o - 1],
            device_id={"seq": seq_at((yi + o) % Y, xi, ci)}, device_id_type=MESH,
        )

    def b_last(o):
        return pltpu.make_async_remote_copy(
            src_ref=tb.at[o - 1], dst_ref=rb3.at[o - 1], send_sem=tbs.at[o - 1], recv_sem=tbr.at[o - 1],
            device_id={"seq": seq_at(yi, (xi + o) % X, ci)}, device_id_type=MESH,
        )

    def for_pair(i):
        oy, ox = ORDER[i]
        j = oy * X + ox
        ga, gb = grads(seq_at((yi + oy) % Y, (xi + ox) % X, ci))
        pair_copy(j).wait_recv()
        for h, p, o in ((0, ox, oy), (1, oy, ox)):
            if p % 2:
                far_copy(h, p // 2, o).wait_recv()
            for w in range(2):
                at = h * half + w * half // 2
                rows = slice(at, at + half // 2)
                va = ga[rows] + r1[j, rows, :depth].astype(F32)
                vb = gb[rows] + r1[j, rows, depth:].astype(F32)
                if p == 1 + 2 * w:
                    va = va + rf[h, w, o, :, :depth].astype(F32)
                    vb = vb + rf[h, w, o, :, depth:].astype(F32)
                to = slice(w * half // 2, (w + 1) * half // 2)
                sg[j, h, to, :depth] = va.astype(BF16)
                sg[j, h, to, depth:] = vb.astype(BF16)
            if p == 2:
                far_copy(h, 0, o).start()
                far_copy(h, 1, o).start()
            elif p:
                near_copy(h, p // 2, o).start()

    tab_copy.wait()
    for r in (2, 6, 1, 7):
        w_copy(r).wait()

    for i in range(8):
        for_sibling(2 * i)
        for_sibling(2 * i + 1)
        if i >= 4:
            for_pair(2 * (i - 4))
            for_pair(2 * (i - 4) + 1)
        event(i % 2, i // 2, 2, False)
    for i in range(8):
        for_pair(8 + i)
        event(i % 2, i // 2, 1, False)

    def branch_block(b):
        v = jnp.dot(lall[b][:, :rank], uv[trial[b]], preferred_element_type=F32)
        branch[b] = ADAPTER_SCALE * v

    loop(blocks, branch_block, 8)

    def column(o):
        for w in range(2):
            near_copy(0, w, o).wait_recv()
            near_copy(1, w, o).wait_recv()
        va, vb = (
            sg[slot_of(h, 0, o), h].astype(F32) + ra[h, 0, o].astype(F32) + ra[h, 1, o].astype(F32) for h in range(2)
        )
        if o == 0:
            fin[0], fin[1] = va, vb
        else:
            ta[o - 1], tb[o - 1] = va.astype(BF16), vb.astype(BF16)
            a_last(o).start()
            b_last(o).start()

    def out_copy(q, i):
        target = seq_at((yi + q + 1) % Y, (xi + i // 2) % X, (ci + i) % C)
        return pltpu.make_async_remote_copy(
            src_ref=mix.at[target], dst_ref=out_h.at[si], send_sem=os.at[q, i], recv_sem=orr.at[q, i],
            device_id={"seq": target}, device_id_type=MESH,
        )

    def out_arrival(q, i):
        source = seq_at((yi + 2 * Y - q - 1) % Y, (xi + X - i // 2) % X, (ci + i) % C)
        return pltpu.make_async_remote_copy(
            src_ref=mix.at[source], dst_ref=out_h.at[source], send_sem=os.at[q, i], recv_sem=orr.at[q, i],
            device_id={"seq": source}, device_id_type=MESH,
        )

    self_copy = pltpu.make_async_copy(mix.at[si], out_h.at[si], loc)
    w_copy(0).wait()

    def finish(q):
        v = own(q, 0)
        for dr in range(2):
            z_copy(dr, q, 1).wait_recv()
        v = v + rbuf[0, q, 0].astype(F32) + rbuf[1, q, 0].astype(F32)
        at = pl.ds(rows_of(q), per)
        mix[at] = (v.reshape(per, blk, cols) + branch[at]).astype(BF16)

        def send(i):
            @pl.when(q * per + i != (CHUNKS - 1) * per)
            def _():
                out_copy(q, i).start()

        loop(per, send)

    column(2)
    column(1)
    finish(0)
    column(3)
    column(0)
    finish(1)
    finish(2)
    finish(3)
    self_copy.start()

    for o in range(1, 4):
        a_last(o).wait_recv()
        b_last(o).wait_recv()
    for h, last in ((0, ra3), (1, rb3)):
        v = fin[h]
        for p in range(3):
            v = v + last[p].astype(F32)
        v = ADAPTER_SCALE * v
        ga_o[0, h * half : (h + 1) * half] = v[:, :depth]
        gb_o[0, h * half : (h + 1) * half] = v[:, depth:]

    def out_wait(n):
        @pl.when(n != (CHUNKS - 1) * per)
        def _():
            out_arrival(n // per, n % per).wait_recv()
            out_copy(n // per, n % per).wait_send()

    loop(blocks, out_wait)
    self_copy.wait()

    loop(4, lambda i: z_copy(i % 2, 2 * (i % 2) + i // 2, 4).wait_send())
    loop(24, lambda i: z_copy(i % 2, (i // 2) % 4, i // 8 + 1).wait_send())
    for o in range(1, Z):
        l_copy(o).wait_send()
        gather_copy(o, zi).wait_send()
    loop(X * Y, lambda j: pair_copy(j).wait_send())
    for o in range(4):
        for w in range(2):
            for h in range(2):
                far_copy(h, w, o).wait_send()
                near_copy(h, w, o).wait_send()
    for o in range(1, 4):
        a_last(o).wait_send()
        b_last(o).wait_send()


def place(out, ga, gb, out_o, ga_o, gb_o):
    out_o[...] = out[...]
    ga_o[...] = ga[...]
    gb_o[...] = gb[...]


def local(x, g, trial_per_block, trial_slot_index, w, down, up):
    blocks = trial_per_block.shape[0]
    trials, depth, rank = down.shape
    cols = up.shape[2]
    blk = x.shape[0] // blocks
    half, wide = rank // 2, depth + cols
    chunk = x.shape[0] // CHUNKS
    hbm = pl.BlockSpec(memory_space=pl.ANY)
    vmem = pl.BlockSpec(memory_space=pltpu.VMEM)
    dma = pltpu.SemaphoreType.DMA
    out, ga, gb = pl.pallas_call(
        kernel,
        out_shape=(
            jax.ShapeDtypeStruct((SEQ, blk, cols), BF16),
            jax.ShapeDtypeStruct((1, rank, depth), F32),
            jax.ShapeDtypeStruct((1, rank, cols), F32),
        ),
        in_specs=[pl.BlockSpec(memory_space=pltpu.SMEM)] * 2 + [vmem] + [hbm] * 5,
        out_specs=(hbm, vmem, vmem),
        scratch_shapes=[
            pltpu.VMEM((trials, 128), jnp.int32),
            pltpu.SMEM((trials, 128), jnp.int32),
            pltpu.VMEM((blocks, blk, depth), BF16),
            pltpu.VMEM((blocks, blk, cols), BF16),
            pltpu.VMEM((Z, depth, cols), BF16),
            pltpu.VMEM((trials, rank, depth), BF16),
            pltpu.VMEM((trials, rank, cols), BF16),
            pltpu.VMEM((2, CHUNKS, 4, chunk, cols), BF16),
            pltpu.VMEM((2, CHUNKS, 4, chunk, cols), BF16),
            pltpu.VMEM((blocks, blk, 2 * rank), F32),
            pltpu.VMEM((blocks, blk, 2 * rank), RANK_SENT),
            pltpu.VMEM((Z - 1, 4, blk, 2 * rank), RANK_SENT),
            pltpu.VMEM((blocks, blk, 2 * rank), BF16),
            pltpu.VMEM((X * Y, rank, wide), BF16),
            pltpu.VMEM((X * Y, rank, wide), BF16),
            pltpu.VMEM((X * Y, 2, half, wide), BF16),
            pltpu.VMEM((2, 2, 4, half // 2, wide), BF16),
            pltpu.VMEM((2, 2, 4, half, wide), BF16),
            pltpu.VMEM((3, half, wide), BF16),
            pltpu.VMEM((3, half, wide), BF16),
            pltpu.VMEM((3, half, wide), BF16),
            pltpu.VMEM((3, half, wide), BF16),
            pltpu.VMEM((2, half, wide), F32),
            pltpu.VMEM((blocks, blk, cols), F32),
            pltpu.VMEM((blocks, blk, cols), BF16),
            dma((13,)),
            dma((2, CHUNKS, 4)), dma((2, CHUNKS, 4)),
            dma((Z - 1,)), dma((Z - 1,)),
            dma((Z - 1,)), dma((Z - 1,)),
            dma((X * Y,)), dma((X * Y,)),
            dma((2, 2, 4)), dma((2, 2, 4)), dma((2, 2, 4)), dma((2, 2, 4)),
            dma((3,)), dma((3,)), dma((3,)), dma((3,)),
            dma((CHUNKS, blocks // CHUNKS)), dma((CHUNKS, blocks // CHUNKS)),
            dma,
        ],
        compiler_params=pltpu.CompilerParams(collective_id=0, has_side_effects=True, vmem_limit_bytes=56 * 2**20),
    )(
        trial_per_block.reshape(blocks), trial_slot_index, trial_per_block.reshape(1, blocks),
        x.reshape(blocks, blk, depth), g.reshape(blocks, blk, cols), w, jnp.transpose(down, (0, 2, 1)), up,
    )
    out, ga, gb = pl.pallas_call(
        place,
        out_shape=tuple(jax.ShapeDtypeStruct(v.shape, v.dtype) for v in (out, ga, gb)),
        in_specs=[vmem] * 3,
        out_specs=(vmem,) * 3,
    )(out, ga, gb)
    return out.reshape(x.shape[0], cols), jnp.transpose(ga, (0, 2, 1)), gb


def solution(mesh):
    in_specs = (
        P("seq", "grp"),
        P("seq", "grp"),
        P("seq", None),
        P(),
        P("grp", None),
        P(None, "grp", None),
        P(None, None, "grp"),
    )
    out_specs = (P("seq", "grp"), P("seq", "grp", None), P("seq", None, "grp"))
    return jax.shard_map(local, mesh=mesh, in_specs=in_specs, out_specs=out_specs, check_vma=False)
```

time: 89.9 us -> 80.3 us (0.89)
  local copies, waits for them, and re-layouts: 6.27 us -> 0 us
  Pallas kernels: 81.7 us -> 79.6 us
  other arithmetic: 0.98 us -> 0 us
    unnamed x3 -> x0, local copies, waits for them, and re-layouts: 5.01 us -> none
    pallas_call x1, Pallas kernels: 81.7 us -> 77.5 us  [local(): pl.pallas_call(kernel, out_shape=(jax.ShapeDtypeStruct((SEQ, blk, cols),...]
    pallas_call x0 -> x1, Pallas kernels: none -> 2.03 us  [local(): pl.pallas_call(place, out_shape=tuple((jax.ShapeDtypeStruct(v.shape, v.dt...]
    another operation x1 -> x0, local copies, waits for them, and re-layouts: 1.26 us -> none  [tables(): jnp.stack([trial, jnp.minimum(first, blocks - 1), jnp.maximum(last, 0), (...]
where the time goes in v3:
time: 80.3 us; the launch traced here: 80.2 us
  Pallas kernels  79.6 us (99%)
    pallas_call x1, Pallas kernels, local(): pl.pallas_call(kernel, out_shape=(jax.ShapeDtypeStruct((SEQ, blk, cols),...  77.5 us
    pallas_call x1, Pallas kernels, local(): pl.pallas_call(place, out_shape=tuple((jax.ShapeDtypeStruct(v.shape, v.dt...  2.03 us

profile of v3, /device:TPU:1, one launch (start us, length us, event | category | flops | bytes accessed | tf_op | source)
XLA Modules:
  0.0 80.2 jit_solution(4886802416085456093)
XLA Ops:
  0.6 77.5 %shard_map.94 = (bf16[32,32,256]{2,1,0:T(8,128)(2,1)}, f32[1,64,1024]{2,1,0:T(8,128)}, f32[1,64,256]{2,1,0:T(8,128)}) custom-call(s32[32]{0:T(128)} %bitcast.10, s32[32]{0:T(128)} %slot.1, s32[1,32]{1,0:T(1,128)} %bitcast.11, bf16[32,32,1024]{2,1,0:T(8,128)(2,1)} %bitcast.8, bf16[32,32,256]{2,1,0:T(8,128)(2,1)} %bitcast.9, bf16[1024,2048]{1,0:T(8,128)(2,1)} %w_h.1, ...), custom_call_target="tpu_custom_call" | custom-call | tf_op jit(solution)/shard_map/pallas_call | solution.py:362
  78.2 2.0 %shard_map.95 = (bf16[32,32,256]{2,1,0:T(8,128)(2,1)}, f32[1,64,1024]{2,1,0:T(8,128)}, f32[1,64,256]{2,1,0:T(8,128)}) custom-call(bf16[32,32,256]{2,1,0:T(8,128)(2,1)} %get-tuple-element.9.out, f32[1,64,1024]{2,1,0:T(8,128)} %get-tuple-element.10.ga, f32[1,64,256]{2,1,0:T(8,128)} %get-tuple-element.11.gb), custom_call_target="tpu_custom_call" | custom-call | tf_op jit(solution)/shard_map/pallas_call | solution.py:412

commit v4 on v3

--- a/solution.py
+++ b/solution.py
@@ -28,7 +28,7 @@
 
 def kernel(
     trial, slot, trial_row, x_h, g_h, w_h, d_h, u_h, out_h, ga_o, gb_o,
-    tab_v, tab, xv, gv, wv, dv, uv, sbuf, rbuf, lp, lsb, lrb, lall, s1, r1, sg, rf, ra, ta, tb, ra3, rb3, fin, branch, mix,
+    tab_v, tab, xv, gv, wv, dv, uv, sbuf, rbuf, lp, lsb, lrb, lall, s1, r1, sg, rf, ra, ta, tb, ra3, rb3, fin, branch, mix, ga_v, gb_v,
     ld_sem, zs, zr, ls, lr, ags, agr, s1s, s1r, rfs, rfr, ras, rar, tas, tar, tbs, tbr, os, orr, loc,
 ):
     zi, si = lax.axis_index("grp"), lax.axis_index("seq")
@@ -77,13 +77,16 @@
             device_id={"grp": (zi + 1 - 2 * dr + Z) % Z}, device_id_type=MESH,
         )
 
-    def event(dr, q, d, first):
-        v = own(q, ((1 - 2 * dr) * d + Z) % Z)
+    def events(places, d, first):
+        sums = [own(q, ((1 - 2 * dr) * d + Z) % Z) for dr, q in enumerate(places)]
         if not first:
-            z_copy(dr, q, d + 1).wait_recv()
-            v = v + rbuf[dr, q, d].astype(F32)
-        sbuf[dr, q, d - 1] = v.astype(BF16)
-        z_copy(dr, q, d).start()
+            for dr, q in enumerate(places):
+                z_copy(dr, q, d + 1).wait_recv()
+            sums = [v + rbuf[dr, q, d].astype(F32) for v, (dr, q) in zip(sums, enumerate(places))]
+        for v, (dr, q) in zip(sums, enumerate(places)):
+            sbuf[dr, q, d - 1] = v.astype(BF16)
+        for dr, q in enumerate(places):
+            z_copy(dr, q, d).start()
 
     def l_copy(o):
         return pltpu.make_async_remote_copy(
@@ -117,7 +120,8 @@
     w_copy(4).wait()
     pl.semaphore_wait(barrier, SEQ - 1 + Z - 1)
 
-    loop(4, lambda i: event(i % 2, 2 * (i % 2) + i // 2, 4, True), 2)
+    for i in range(2):
+        events((i, 2 + i), 4, True)
 
     d_copy.wait()
     g_copy.wait()
@@ -136,7 +140,8 @@
         l_copy(o).start()
     for r in (3, 5):
         w_copy(r).wait()
-    loop(4, lambda i: event(i % 2, 2 * (1 - i % 2) + i // 2, 3, True), 2)
+    for i in range(2):
+        events((2 + i, i), 3, True)
     mine = pl.ds(zi * 4, 4)
     v = lp[mine]
     for o in range(1, Z):
@@ -145,7 +150,8 @@
     lall[mine] = v.astype(BF16)
     for o in (4, 3, 5, 2, 6, 1, 7):
         gather_copy(o, zi).start()
-    loop(4, lambda i: event(i % 2, 2 * (i % 2) + i // 2, 3, False), 2)
+    for i in range(2):
+        events((i, 2 + i), 3, False)
 
     for o in range(1, Z):
         gather_copy(o, (zi - o + Z) % Z).wait_recv()
@@ -167,13 +173,14 @@
             device_id={"seq": seq_at(yi, xi, 1 - ci)}, device_id_type=MESH,
         )
 
-    def for_sibling(i):
-        oy, ox = ORDER[i]
-        j = oy * X + ox
-        ga, gb = grads(seq_at((yi + oy) % Y, (xi + ox) % X, 1 - ci))
-        s1[j, :, :depth] = ga.astype(BF16)
-        s1[j, :, depth:] = gb.astype(BF16)
-        pair_copy(j).start()
+    def for_sibling(turns):
+        places = [ORDER[i] for i in turns]
+        made = [grads(seq_at((yi + oy) % Y, (xi + ox) % X, 1 - ci)) for oy, ox in places]
+        for (oy, ox), (ga, gb) in zip(places, made):
+            s1[oy * X + ox, :, :depth] = ga.astype(BF16)
+            s1[oy * X + ox, :, depth:] = gb.astype(BF16)
+        for oy, ox in places:
+            pair_copy(oy * X + ox).start()
 
     def slot_of(h, p, o):
         return o * X + p if h == 0 else p * X + o
@@ -205,14 +212,17 @@
             device_id={"seq": seq_at(yi, (xi + o) % X, ci)}, device_id_type=MESH,
         )
 
-    def for_pair(i):
-        oy, ox = ORDER[i]
-        j = oy * X + ox
-        ga, gb = grads(seq_at((yi + oy) % Y, (xi + ox) % X, ci))
-        pair_copy(j).wait_recv()
-        for h, p, o in ((0, ox, oy), (1, oy, ox)):
+    def for_pair(turns):
+        places = [ORDER[i] for i in turns]
+        parts = [(j, h, p, o) for j, oy, ox in [(y * X + x, y, x) for y, x in places] for h, p, o in ((0, ox, oy), (1, oy, ox))]
+        made = {oy * X + ox: grads(seq_at((yi + oy) % Y, (xi + ox) % X, ci)) for oy, ox in places}
+        for j in made:
+            pair_copy(j).wait_recv()
+        for j, h, p, o in parts:
             if p % 2:
                 far_copy(h, p // 2, o).wait_recv()
+        for j, h, p, o in parts:
+            ga, gb = made[j]
             for w in range(2):
                 at = h * half + w * half // 2
                 rows = slice(at, at + half // 2)
@@ -224,6 +234,7 @@
                 to = slice(w * half // 2, (w + 1) * half // 2)
                 sg[j, h, to, :depth] = va.astype(BF16)
                 sg[j, h, to, depth:] = vb.astype(BF16)
+        for j, h, p, o in parts:
             if p == 2:
                 far_copy(h, 0, o).start()
                 far_copy(h, 1, o).start()
@@ -235,15 +246,13 @@
         w_copy(r).wait()
 
     for i in range(8):
-        for_sibling(2 * i)
-        for_sibling(2 * i + 1)
-        if i >= 4:
-            for_pair(2 * (i - 4))
-            for_pair(2 * (i - 4) + 1)
-        event(i % 2, i // 2, 2, False)
-    for i in range(8):
-        for_pair(8 + i)
-        event(i % 2, i // 2, 1, False)
+        for_sibling(range(2 * i, 2 * i + 2))
+    for i in range(4):
+        for_pair(range(2 * i, 2 * i + 2))
+        events((i, i), 2, False)
+    for i in range(4):
+        for_pair(range(8 + 2 * i, 10 + 2 * i))
+        events((i, i), 1, False)
 
     def branch_block(b):
         v = jnp.dot(lall[b][:, :rank], uv[trial[b]], preferred_element_type=F32)
@@ -279,7 +288,7 @@
             device_id={"seq": source}, device_id_type=MESH,
         )
 
-    self_copy = pltpu.make_async_copy(mix.at[si], out_h.at[si], loc)
+    self_copy = pltpu.make_async_copy(mix.at[si], out_h.at[si], loc.at[0])
     w_copy(0).wait()
 
     def finish(q):
@@ -315,17 +324,12 @@
         for p in range(3):
             v = v + last[p].astype(F32)
         v = ADAPTER_SCALE * v
-        ga_o[0, h * half : (h + 1) * half] = v[:, :depth]
-        gb_o[0, h * half : (h + 1) * half] = v[:, depth:]
-
-    def out_wait(n):
-        @pl.when(n != (CHUNKS - 1) * per)
-        def _():
-            out_arrival(n // per, n % per).wait_recv()
-            out_copy(n // per, n % per).wait_send()
-
-    loop(blocks, out_wait)
-    self_copy.wait()
+        ga_v[h * half : (h + 1) * half] = v[:, :depth]
+        gb_v[h * half : (h + 1) * half] = v[:, depth:]
+    ga_copy = pltpu.make_async_copy(ga_v, ga_o.at[0], loc.at[1])
+    gb_copy = pltpu.make_async_copy(gb_v, gb_o.at[0], loc.at[2])
+    ga_copy.start()
+    gb_copy.start()
 
     loop(4, lambda i: z_copy(i % 2, 2 * (i % 2) + i // 2, 4).wait_send())
     loop(24, lambda i: z_copy(i % 2, (i // 2) % 4, i // 8 + 1).wait_send())
@@ -341,6 +345,17 @@
     for o in range(1, 4):
         a_last(o).wait_send()
         b_last(o).wait_send()
+
+    def out_wait(n):
+        @pl.when(n != (CHUNKS - 1) * per)
+        def _():
+            out_copy(n // per, n % per).wait_send()
+            out_arrival(n // per, n % per).wait_recv()
+
+    loop(blocks, out_wait)
+    self_copy.wait()
+    ga_copy.wait()
+    gb_copy.wait()
 
 
 def place(out, ga, gb, out_o, ga_o, gb_o):
@@ -367,7 +382,7 @@
             jax.ShapeDtypeStruct((1, rank, cols), F32),
         ),
         in_specs=[pl.BlockSpec(memory_space=pltpu.SMEM)] * 2 + [vmem] + [hbm] * 5,
-        out_specs=(hbm, vmem, vmem),
+        out_specs=(hbm,) * 3,
         scratch_shapes=[
             pltpu.VMEM((trials, 128), jnp.int32),
             pltpu.SMEM((trials, 128), jnp.int32),
@@ -394,6 +409,8 @@
             pltpu.VMEM((2, half, wide), F32),
             pltpu.VMEM((blocks, blk, cols), F32),
             pltpu.VMEM((blocks, blk, cols), BF16),
+            pltpu.VMEM((rank, depth), F32),
+            pltpu.VMEM((rank, cols), F32),
             dma((13,)),
             dma((2, CHUNKS, 4)), dma((2, CHUNKS, 4)),
             dma((Z - 1,)), dma((Z - 1,)),
@@ -402,7 +419,7 @@
             dma((2, 2, 4)), dma((2, 2, 4)), dma((2, 2, 4)), dma((2, 2, 4)),
             dma((3,)), dma((3,)), dma((3,)), dma((3,)),
             dma((CHUNKS, blocks // CHUNKS)), dma((CHUNKS, blocks // CHUNKS)),
-            dma,
+            dma((3,)),
         ],
         compiler_params=pltpu.CompilerParams(collective_id=0, has_side_effects=True, vmem_limit_bytes=56 * 2**20),
     )(

time: 80.3 us -> 75.5 us (0.940)
  Pallas kernels: 79.6 us -> 74.7 us
    pallas_call x1, Pallas kernels: 77.5 us -> 72.7 us  [local(): pl.pallas_call(kernel, out_shape=(jax.ShapeDtypeStruct((SEQ, blk, cols),...]
where the time goes in v4:
time: 75.5 us; the launch traced here: 75.4 us
  Pallas kernels  74.7 us (99%)
    pallas_call x1, Pallas kernels, local(): pl.pallas_call(kernel, out_shape=(jax.ShapeDtypeStruct((SEQ, blk, cols),...  72.7 us
    pallas_call x1, Pallas kernels, local(): pl.pallas_call(place, out_shape=tuple((jax.ShapeDtypeStruct(v.shape, v.dt...  2.03 us

profile of v4, /device:TPU:1, one launch (start us, length us, event | category | flops | bytes accessed | tf_op | source)
XLA Modules:
  0.0 75.4 jit_solution(1831776756573211555)
XLA Ops:
  0.6 72.7 %shard_map.94 = (bf16[32,32,256]{2,1,0:T(8,128)(2,1)}, f32[1,64,1024]{2,1,0:T(8,128)}, f32[1,64,256]{2,1,0:T(8,128)}) custom-call(s32[32]{0:T(128)} %bitcast.10, s32[32]{0:T(128)} %slot.1, s32[1,32]{1,0:T(1,128)} %bitcast.11, bf16[32,32,1024]{2,1,0:T(8,128)(2,1)} %bitcast.8, bf16[32,32,256]{2,1,0:T(8,128)(2,1)} %bitcast.9, bf16[1024,2048]{1,0:T(8,128)(2,1)} %w_h.1, ...), custom_call_target="tpu_custom_call" | custom-call | tf_op jit(solution)/shard_map/pallas_call | solution.py:377
  73.3 2.0 %shard_map.95 = (bf16[32,32,256]{2,1,0:T(8,128)(2,1)}, f32[1,64,1024]{2,1,0:T(8,128)}, f32[1,64,256]{2,1,0:T(8,128)}) custom-call(bf16[32,32,256]{2,1,0:T(8,128)(2,1)} %get-tuple-element.9.out, f32[1,64,1024]{2,1,0:T(8,128)} %get-tuple-element.10.ga, f32[1,64,256]{2,1,0:T(8,128)} %get-tuple-element.11.gb), custom_call_target="tpu_custom_call" | custom-call | tf_op jit(solution)/shard_map/pallas_call | solution.py:429

commit v5 on v4

--- a/solution.py
+++ b/solution.py
@@ -118,10 +118,11 @@
 
     x_copy.wait()
     w_copy(4).wait()
+    for q in range(CHUNKS):
+        sbuf[q // 2, q, 3] = own(q, 4).astype(BF16)
     pl.semaphore_wait(barrier, SEQ - 1 + Z - 1)
-
-    for i in range(2):
-        events((i, 2 + i), 4, True)
+    for q in (0, 2, 1, 3):
+        z_copy(q // 2, q, 4).start()
 
     d_copy.wait()
     g_copy.wait()
@@ -248,11 +249,11 @@
     for i in range(8):
         for_sibling(range(2 * i, 2 * i + 2))
     for i in range(4):
+        events((i, i), 2, False)
         for_pair(range(2 * i, 2 * i + 2))
-        events((i, i), 2, False)
     for i in range(4):
+        events((i, i), 1, False)
         for_pair(range(8 + 2 * i, 10 + 2 * i))
-        events((i, i), 1, False)
 
     def branch_block(b):
         v = jnp.dot(lall[b][:, :rank], uv[trial[b]], preferred_element_type=F32)
@@ -358,10 +359,17 @@
     gb_copy.wait()
 
 
-def place(out, ga, gb, out_o, ga_o, gb_o):
-    out_o[...] = out[...]
-    ga_o[...] = ga[...]
-    gb_o[...] = gb[...]
+def place(out, ga, gb, out_o, ga_o, gb_o, out_v, ga_v, gb_v, get, put):
+    ways = ((out, out_v, out_o), (ga, ga_v, ga_o), (gb, gb_v, gb_o))
+    gets = [pltpu.make_async_copy(a, v, get.at[i]) for i, (a, v, b) in enumerate(ways)]
+    puts = [pltpu.make_async_copy(v, b, put.at[i]) for i, (a, v, b) in enumerate(ways)]
+    for copy in gets:
+        copy.start()
+    for i in range(3):
+        gets[i].wait()
+        puts[i].start()
+    for copy in puts:
+        copy.wait()
 
 
 def local(x, g, trial_per_block, trial_slot_index, w, down, up):
@@ -429,8 +437,9 @@
     out, ga, gb = pl.pallas_call(
         place,
         out_shape=tuple(jax.ShapeDtypeStruct(v.shape, v.dtype) for v in (out, ga, gb)),
-        in_specs=[vmem] * 3,
-        out_specs=(vmem,) * 3,
+        in_specs=[hbm] * 3,
+        out_specs=(hbm,) * 3,
+        scratch_shapes=[pltpu.VMEM(v.shape, v.dtype) for v in (out, ga, gb)] + [dma((3,)), dma((3,))],
     )(out, ga, gb)
     return out.reshape(x.shape[0], cols), jnp.transpose(ga, (0, 2, 1)), gb
 

time: 75.5 us -> 74.2 us (0.983)
  Pallas kernels: 74.7 us -> 73.4 us
    pallas_call x1, Pallas kernels: 72.7 us -> 71.5 us  [local(): pl.pallas_call(kernel, out_shape=(jax.ShapeDtypeStruct((SEQ, blk, cols),...]
where the time goes in v5:
time: 74.2 us; the launch traced here: 74.1 us
  Pallas kernels  73.4 us (99%)
    pallas_call x1, Pallas kernels, local(): pl.pallas_call(kernel, out_shape=(jax.ShapeDtypeStruct((SEQ, blk, cols),...  71.5 us
    pallas_call x1, Pallas kernels, local(): pl.pallas_call(place, out_shape=tuple((jax.ShapeDtypeStruct(v.shape, v.dt...  1.98 us

profile of v5, /device:TPU:1, one launch (start us, length us, event | category | flops | bytes accessed | tf_op | source)
XLA Modules:
  0.0 74.1 jit_solution(11501306084932575906)
XLA Ops:
  0.6 71.5 %shard_map.94 = (bf16[32,32,256]{2,1,0:T(8,128)(2,1)}, f32[1,64,1024]{2,1,0:T(8,128)}, f32[1,64,256]{2,1,0:T(8,128)}) custom-call(s32[32]{0:T(128)} %bitcast.10, s32[32]{0:T(128)} %slot.1, s32[1,32]{1,0:T(1,128)} %bitcast.11, bf16[32,32,1024]{2,1,0:T(8,128)(2,1)} %bitcast.8, bf16[32,32,256]{2,1,0:T(8,128)(2,1)} %bitcast.9, bf16[1024,2048]{1,0:T(8,128)(2,1)} %w_h.1, ...), custom_call_target="tpu_custom_call" | custom-call | tf_op jit(solution)/shard_map/pallas_call | solution.py:385
  72.1 2.0 %shard_map.95 = (bf16[32,32,256]{2,1,0:T(8,128)(2,1)}, f32[1,64,1024]{2,1,0:T(8,128)}, f32[1,64,256]{2,1,0:T(8,128)}) custom-call(bf16[32,32,256]{2,1,0:T(8,128)(2,1)} %get-tuple-element.9.out, f32[1,64,1024]{2,1,0:T(8,128)} %get-tuple-element.10.ga, f32[1,64,256]{2,1,0:T(8,128)} %get-tuple-element.11.gb), custom_call_target="tpu_custom_call" | custom-call | tf_op jit(solution)/shard_map/pallas_call | solution.py:437

commit v6 on v5

--- a/solution.py
+++ b/solution.py
@@ -128,23 +128,28 @@
     g_copy.wait()
     u_copy.wait()
 
-    def rank_block(b):
-        t = trial[b]
-        down = lax.dot_general(xv[b], dv[t], NT, preferred_element_type=F32)
-        back = lax.dot_general(gv[b], uv[t], NT, preferred_element_type=F32)
-        v = jnp.concatenate([down, back], axis=1)
-        lp[b] = v
-        lsb[b] = v.astype(lsb.dtype)
-
-    loop(blocks, rank_block, 8)
+    def rank_sums(o):
+        made = []
+        for n in range(4):
+            b = ((zi + o) % Z) * 4 + n
+            t = trial[b]
+            down = lax.dot_general(xv[b], dv[t], NT, preferred_element_type=F32)
+            back = lax.dot_general(gv[b], uv[t], NT, preferred_element_type=F32)
+            made.append(jnp.concatenate([down, back], axis=1))
+        return made
+
     for o in (4, 3, 5, 2, 6, 1, 7):
+        for n, v in enumerate(rank_sums(o)):
+            lsb[((zi + o) % Z) * 4 + n] = v.astype(RANK_SENT)
         l_copy(o).start()
+    for n, v in enumerate(rank_sums(0)):
+        lp[n] = v
     for r in (3, 5):
         w_copy(r).wait()
     for i in range(2):
         events((2 + i, i), 3, True)
     mine = pl.ds(zi * 4, 4)
-    v = lp[mine]
+    v = lp[...]
     for o in range(1, Z):
         l_copy(o).wait_recv()
         v = v + lrb[o - 1].astype(F32)
@@ -242,6 +247,20 @@
             elif p:
                 near_copy(h, p // 2, o).start()
 
+    def column(o):
+        for w in range(2):
+            near_copy(0, w, o).wait_recv()
+            near_copy(1, w, o).wait_recv()
+        va, vb = (
+            sg[slot_of(h, 0, o), h].astype(F32) + ra[h, 0, o].astype(F32) + ra[h, 1, o].astype(F32) for h in range(2)
+        )
+        if o == 0:
+            fin[0], fin[1] = va, vb
+        else:
+            ta[o - 1], tb[o - 1] = va.astype(BF16), vb.astype(BF16)
+            a_last(o).start()
+            b_last(o).start()
+
     tab_copy.wait()
     for r in (2, 6, 1, 7):
         w_copy(r).wait()
@@ -254,26 +273,14 @@
     for i in range(4):
         events((i, i), 1, False)
         for_pair(range(8 + 2 * i, 10 + 2 * i))
+        if i:
+            column((0, 2, 1, 3)[i])
 
     def branch_block(b):
         v = jnp.dot(lall[b][:, :rank], uv[trial[b]], preferred_element_type=F32)
         branch[b] = ADAPTER_SCALE * v
 
     loop(blocks, branch_block, 8)
-
-    def column(o):
-        for w in range(2):
-            near_copy(0, w, o).wait_recv()
-            near_copy(1, w, o).wait_recv()
-        va, vb = (
-            sg[slot_of(h, 0, o), h].astype(F32) + ra[h, 0, o].astype(F32) + ra[h, 1, o].astype(F32) for h in range(2)
-        )
-        if o == 0:
-            fin[0], fin[1] = va, vb
-        else:
-            ta[o - 1], tb[o - 1] = va.astype(BF16), vb.astype(BF16)
-            a_last(o).start()
-            b_last(o).start()
 
     def out_copy(q, i):
         target = seq_at((yi + q + 1) % Y, (xi + i // 2) % X, (ci + i) % C)
@@ -307,10 +314,7 @@
 
         loop(per, send)
 
-    column(2)
-    column(1)
     finish(0)
-    column(3)
     column(0)
     finish(1)
     finish(2)
@@ -401,7 +405,7 @@
             pltpu.VMEM((trials, rank, cols), BF16),
             pltpu.VMEM((2, CHUNKS, 4, chunk, cols), BF16),
             pltpu.VMEM((2, CHUNKS, 4, chunk, cols), BF16),
-            pltpu.VMEM((blocks, blk, 2 * rank), F32),
+            pltpu.VMEM((4, blk, 2 * rank), F32),
             pltpu.VMEM((blocks, blk, 2 * rank), RANK_SENT),
             pltpu.VMEM((Z - 1, 4, blk, 2 * rank), RANK_SENT),
             pltpu.VMEM((blocks, blk, 2 * rank), BF16),

time: 74.2 us -> 74.7 us (level)
  no operation moved by 1% of the time
where the time goes in v6:
time: 74.7 us; the launch traced here: 74.6 us
  Pallas kernels  73.9 us (99%)
    pallas_call x1, Pallas kernels, local(): pl.pallas_call(kernel, out_shape=(jax.ShapeDtypeStruct((SEQ, blk, cols),...  72 us
    pallas_call x1, Pallas kernels, local(): pl.pallas_call(place, out_shape=tuple((jax.ShapeDtypeStruct(v.shape, v.dt...  1.98 us

profile of v6, /device:TPU:1, one launch (start us, length us, event | category | flops | bytes accessed | tf_op | source)
XLA Modules:
  0.0 74.6 jit_solution(10273523689908344096)
XLA Ops:
  0.6 72.0 %shard_map.94 = (bf16[32,32,256]{2,1,0:T(8,128)(2,1)}, f32[1,64,1024]{2,1,0:T(8,128)}, f32[1,64,256]{2,1,0:T(8,128)}) custom-call(s32[32]{0:T(128)} %bitcast.10, s32[32]{0:T(128)} %slot.1, s32[1,32]{1,0:T(1,128)} %bitcast.11, bf16[32,32,1024]{2,1,0:T(8,128)(2,1)} %bitcast.8, bf16[32,32,256]{2,1,0:T(8,128)(2,1)} %bitcast.9, bf16[1024,2048]{1,0:T(8,128)(2,1)} %w_h.1, ...), custom_call_target="tpu_custom_call" | custom-call | tf_op jit(solution)/shard_map/pallas_call | solution.py:389
  72.6 2.0 %shard_map.95 = (bf16[32,32,256]{2,1,0:T(8,128)(2,1)}, f32[1,64,1024]{2,1,0:T(8,128)}, f32[1,64,256]{2,1,0:T(8,128)}) custom-call(bf16[32,32,256]{2,1,0:T(8,128)(2,1)} %get-tuple-element.9.out, f32[1,64,1024]{2,1,0:T(8,128)} %get-tuple-element.10.ga, f32[1,64,256]{2,1,0:T(8,128)} %get-tuple-element.11.gb), custom_call_target="tpu_custom_call" | custom-call | tf_op jit(solution)/shard_map/pallas_call | solution.py:441

commit v7 on v6

--- a/solution.py
+++ b/solution.py
@@ -91,14 +91,14 @@
     def l_copy(o):
         return pltpu.make_async_remote_copy(
             src_ref=lsb.at[pl.ds(((zi + o) % Z) * 4, 4)], dst_ref=lrb.at[o - 1], send_sem=ls.at[o - 1], recv_sem=lr.at[o - 1],
-            device_id={"grp": (zi + o) % Z}, device_id_type=MESH,
+            device_id={"grp": (zi + (1 if o == 4 else o)) % Z}, device_id_type=MESH,
         )
 
     def gather_copy(o, source):
         at = pl.ds(source * 4, 4)
         return pltpu.make_async_remote_copy(
             src_ref=lall.at[at], dst_ref=lall.at[at], send_sem=ags.at[o - 1], recv_sem=agr.at[o - 1],
-            device_id={"grp": (zi + o) % Z}, device_id_type=MESH,
+            device_id={"grp": (zi + (7 if o == 4 else o)) % Z}, device_id_type=MESH,
         )
 
     count = slot.shape[0]
@@ -138,28 +138,35 @@
             made.append(jnp.concatenate([down, back], axis=1))
         return made
 
-    for o in (4, 3, 5, 2, 6, 1, 7):
+    for o in (4, 5, 2, 6, 1, 7):
         for n, v in enumerate(rank_sums(o)):
             lsb[((zi + o) % Z) * 4 + n] = v.astype(RANK_SENT)
         l_copy(o).start()
     for n, v in enumerate(rank_sums(0)):
         lp[n] = v
+    made = rank_sums(3)
+    l_copy(4).wait_recv()
+    for n, v in enumerate(made):
+        lsb[((zi + 3) % Z) * 4 + n] = (v + lrb[3, n].astype(F32)).astype(RANK_SENT)
+    l_copy(3).start()
     for r in (3, 5):
         w_copy(r).wait()
     for i in range(2):
         events((2 + i, i), 3, True)
     mine = pl.ds(zi * 4, 4)
     v = lp[...]
-    for o in range(1, Z):
+    for o in (1, 2, 3, 5, 6, 7):
         l_copy(o).wait_recv()
         v = v + lrb[o - 1].astype(F32)
     lall[mine] = v.astype(BF16)
-    for o in (4, 3, 5, 2, 6, 1, 7):
+    for o in (5, 3, 2, 6, 1, 7):
         gather_copy(o, zi).start()
     for i in range(2):
         events((i, 2 + i), 3, False)
 
-    for o in range(1, Z):
+    gather_copy(5, (zi + 3) % Z).wait_recv()
+    gather_copy(4, (zi + 3) % Z).start()
+    for o in (1, 2, 3, 6, 7, 4):
         gather_copy(o, (zi - o + Z) % Z).wait_recv()
 
     def grads(k):
@@ -273,8 +280,6 @@
     for i in range(4):
         events((i, i), 1, False)
         for_pair(range(8 + 2 * i, 10 + 2 * i))
-        if i:
-            column((0, 2, 1, 3)[i])
 
     def branch_block(b):
         v = jnp.dot(lall[b][:, :rank], uv[trial[b]], preferred_element_type=F32)
@@ -314,7 +319,10 @@
 
         loop(per, send)
 
+    column(2)
+    column(1)
     finish(0)
+    column(3)
     column(0)
     finish(1)
     finish(2)
@@ -340,7 +348,7 @@
     loop(24, lambda i: z_copy(i % 2, (i // 2) % 4, i // 8 + 1).wait_send())
     for o in range(1, Z):
         l_copy(o).wait_send()
-        gather_copy(o, zi).wait_send()
+        gather_copy(o, (zi + 3) % Z if o == 4 else zi).wait_send()
     loop(X * Y, lambda j: pair_copy(j).wait_send())
     for o in range(4):
         for w in range(2):

time: 74.7 us -> 75.6 us (1.012)
  Pallas kernels: 73.9 us -> 74.9 us
    pallas_call x1, Pallas kernels: 72 us -> 72.9 us  [local(): pl.pallas_call(kernel, out_shape=(jax.ShapeDtypeStruct((SEQ, blk, cols),...]
where the time goes in v7:
time: 75.6 us; the launch traced here: 75.5 us
  Pallas kernels  74.9 us (99%)
    pallas_call x1, Pallas kernels, local(): pl.pallas_call(kernel, out_shape=(jax.ShapeDtypeStruct((SEQ, blk, cols),...  72.9 us
    pallas_call x1, Pallas kernels, local(): pl.pallas_call(place, out_shape=tuple((jax.ShapeDtypeStruct(v.shape, v.dt...  1.98 us

profile of v7, /device:TPU:1, one launch (start us, length us, event | category | flops | bytes accessed | tf_op | source)
XLA Modules:
  0.0 75.5 jit_solution(2757113166534159957)
XLA Ops:
  0.6 72.9 %shard_map.94 = (bf16[32,32,256]{2,1,0:T(8,128)(2,1)}, f32[1,64,1024]{2,1,0:T(8,128)}, f32[1,64,256]{2,1,0:T(8,128)}) custom-call(s32[32]{0:T(128)} %bitcast.10, s32[32]{0:T(128)} %slot.1, s32[1,32]{1,0:T(1,128)} %bitcast.11, bf16[32,32,1024]{2,1,0:T(8,128)(2,1)} %bitcast.8, bf16[32,32,256]{2,1,0:T(8,128)(2,1)} %bitcast.9, bf16[1024,2048]{1,0:T(8,128)(2,1)} %w_h.1, ...), custom_call_target="tpu_custom_call" | custom-call | tf_op jit(solution)/shard_map/pallas_call | solution.py:397
  73.5 2.0 %shard_map.95 = (bf16[32,32,256]{2,1,0:T(8,128)(2,1)}, f32[1,64,1024]{2,1,0:T(8,128)}, f32[1,64,256]{2,1,0:T(8,128)}) custom-call(bf16[32,32,256]{2,1,0:T(8,128)(2,1)} %get-tuple-element.9.out, f32[1,64,1024]{2,1,0:T(8,128)} %get-tuple-element.10.ga, f32[1,64,256]{2,1,0:T(8,128)} %get-tuple-element.11.gb), custom_call_target="tpu_custom_call" | custom-call | tf_op jit(solution)/shard_map/pallas_call | solution.py:449

commit v8 on v6

--- a/solution.py
+++ b/solution.py
@@ -146,8 +146,7 @@
         lp[n] = v
     for r in (3, 5):
         w_copy(r).wait()
-    for i in range(2):
-        events((2 + i, i), 3, True)
+    events((2, 0), 3, True)
     mine = pl.ds(zi * 4, 4)
     v = lp[...]
     for o in range(1, Z):
@@ -156,6 +155,7 @@
     lall[mine] = v.astype(BF16)
     for o in (4, 3, 5, 2, 6, 1, 7):
         gather_copy(o, zi).start()
+    events((3, 1), 3, True)
     for i in range(2):
         events((i, 2 + i), 3, False)
 
@@ -273,8 +273,6 @@
     for i in range(4):
         events((i, i), 1, False)
         for_pair(range(8 + 2 * i, 10 + 2 * i))
-        if i:
-            column((0, 2, 1, 3)[i])
 
     def branch_block(b):
         v = jnp.dot(lall[b][:, :rank], uv[trial[b]], preferred_element_type=F32)
@@ -314,7 +312,10 @@
 
         loop(per, send)
 
+    column(2)
+    column(1)
     finish(0)
+    column(3)
     column(0)
     finish(1)
     finish(2)

time: 74.7 us -> 74.2 us (level)
  no operation moved by 1% of the time
where the time goes in v8:
time: 74.2 us; the launch traced here: 74.1 us
  Pallas kernels  73.5 us (99%)
    pallas_call x1, Pallas kernels, local(): pl.pallas_call(kernel, out_shape=(jax.ShapeDtypeStruct((SEQ, blk, cols),...  71.5 us
    pallas_call x1, Pallas kernels, local(): pl.pallas_call(place, out_shape=tuple((jax.ShapeDtypeStruct(v.shape, v.dt...  1.98 us

profile of v8, /device:TPU:1, one launch (start us, length us, event | category | flops | bytes accessed | tf_op | source)
XLA Modules:
  0.0 74.1 jit_solution(12956108454873321638)
XLA Ops:
  0.6 71.5 %shard_map.94 = (bf16[32,32,256]{2,1,0:T(8,128)(2,1)}, f32[1,64,1024]{2,1,0:T(8,128)}, f32[1,64,256]{2,1,0:T(8,128)}) custom-call(s32[32]{0:T(128)} %bitcast.10, s32[32]{0:T(128)} %slot.1, s32[1,32]{1,0:T(1,128)} %bitcast.11, bf16[32,32,1024]{2,1,0:T(8,128)(2,1)} %bitcast.8, bf16[32,32,256]{2,1,0:T(8,128)(2,1)} %bitcast.9, bf16[1024,2048]{1,0:T(8,128)(2,1)} %w_h.1, ...), custom_call_target="tpu_custom_call" | custom-call | tf_op jit(solution)/shard_map/pallas_call | solution.py:390
  72.1 2.0 %shard_map.95 = (bf16[32,32,256]{2,1,0:T(8,128)(2,1)}, f32[1,64,1024]{2,1,0:T(8,128)}, f32[1,64,256]{2,1,0:T(8,128)}) custom-call(bf16[32,32,256]{2,1,0:T(8,128)(2,1)} %get-tuple-element.9.out, f32[1,64,1024]{2,1,0:T(8,128)} %get-tuple-element.10.ga, f32[1,64,256]{2,1,0:T(8,128)} %get-tuple-element.11.gb), custom_call_target="tpu_custom_call" | custom-call | tf_op jit(solution)/shard_map/pallas_call | solution.py:442
